TPU v7x, 512 devices: a whole 4x8x8 slice. The times are simulated.
512 devices in a mesh: wide: 64 (over y, x, core), narrow: 8 (over z).
Axes of the slice: x: 4, y: 8, z: 8, core: 2. Of those that a mesh axis runs over, the one named last changes fastest.
Arguments:
- amplitudes: bfloat16 [256, 128, 4096], P('wide', None, 'narrow'), may hold values from -6 to 6
- int_values: bfloat16 [192, 4096], P('narrow'), may hold values from -0.5 to 0.5
- hole_ladder: bfloat16 [256, 256], replicated, may hold values from -0.375 to 0.375
- amp_tiles: int32 [128], replicated, may hold values from 0 to 575, as said below
- int_tiles: int32 [192], replicated, may hold values from 0 to 575, as said below
- owner: int32 [128, 1], replicated, may hold values from 0 to 63; in each aligned block of 128 rows (0 to 127, 128 to 255, ...) at most 4 rows name the same one
Outputs:
- residual: bfloat16 [256, 256, 4096], P(None, 'wide', 'narrow')
Inputs may be any that keep to these rules, and one draw needn't show every extreme that they name: `amp_tiles`: 128 distinct codes, each first tile * 24 + second tile; no first tile has more than 6 codes, and some first tile has exactly 6. `int_tiles`: 192 distinct codes, each first tile * 24 + second tile; codes 0 and 575 are always among them. `owner`: every index of wide owns at least one and at most 4 amplitude tiles; some index owns exactly 4.
All inputs are finite; a program needn't handle non-finite values.
Results may differ from a plain program's by a relative error of at most 0.0038.
Values may be sent and summed in bfloat16 or wider, within the bound.
A program may use at most 128 MiB of HBM per device.

v0:
```python
import jax
import jax.numpy as jnp
from jax import lax
from jax.sharding import PartitionSpec as P

TILE = 64
NVT = 24
CAP = 4


def tile_table(tile_codes, list_length):
    codes_grid = jnp.arange(NVT * NVT, dtype=jnp.int32)
    matches = codes_grid[:, None] == tile_codes[None, :]
    number = jnp.arange(list_length, dtype=jnp.int32)
    located = jnp.sum(jnp.where(matches, number[None, :], 0), axis=1)
    present = jnp.any(matches, axis=1)
    return jnp.where(present, located, list_length).reshape(NVT, NVT)


def slot_table(owner, list_length, slot_count):
    owners = owner[:, 0]
    number = jnp.arange(list_length, dtype=jnp.int32)
    earlier = (owners[:, None] == owners[None, :]) & (number[None, :] < number[:, None])
    earlier_count = jnp.sum(earlier.astype(jnp.int32), axis=1)
    position = owners * CAP + earlier_count
    slot_ids = jnp.arange(slot_count, dtype=jnp.int32)
    matches = slot_ids[:, None] == position[None, :]
    located = jnp.sum(jnp.where(matches, number[None, :], 0), axis=1)
    return jnp.where(jnp.any(matches, axis=1), located, list_length)


def row_lists(amp_table, tile_count, row_most):
    present = amp_table < tile_count
    place = jnp.cumsum(present.astype(jnp.int32), axis=1) - 1
    slot_numbers = jnp.arange(row_most, dtype=jnp.int32)
    hits = present[:, None, :] & (place[:, None, :] == slot_numbers[None, :, None])
    found = jnp.any(hits, axis=2)
    tile_ids = jnp.sum(jnp.where(hits, amp_table[:, None, :], 0), axis=2)
    column_ids = jnp.arange(NVT, dtype=jnp.int32)
    second_ids = jnp.sum(jnp.where(hits, column_ids[None, None, :], 0), axis=2)
    return (jnp.where(found, tile_ids, tile_count), second_ids, found, place)


def per_device(amplitudes, int_values, hole_ladder, amp_tiles, int_tiles, owner):
    pair_rows, tile_count, row_cells = amplitudes.shape
    wide_size = lax.axis_size("wide")
    rows_local = row_cells // TILE
    row_most = (tile_count + NVT - 1) // NVT
    slot_ids = slot_table(owner, tile_count, wide_size * CAP)
    by_tile = jnp.transpose(amplitudes, (1, 0, 2))
    by_tile = jnp.concatenate(
        [by_tile, jnp.zeros((1, pair_rows, row_cells), by_tile.dtype)], axis=0
    )
    send_amps = jnp.transpose(by_tile[slot_ids], (1, 0, 2)).reshape(
        pair_rows, wide_size, CAP, row_cells
    )
    int_all = lax.all_gather(int_values, "narrow", axis=0, tiled=True)
    int_count = int_all.shape[0]
    int_pad = jnp.concatenate([int_all, jnp.zeros((1, TILE * TILE), int_all.dtype)], axis=0)
    amp_table = tile_table(amp_tiles, tile_count)
    int_table = tile_table(int_tiles, int_count)
    tile_lists, second_lists, found_lists, place = row_lists(amp_table, tile_count, row_most)
    left_tiles = by_tile[tile_lists].reshape(NVT, row_most, pair_rows, rows_local, TILE)
    left_matrix = jnp.transpose(left_tiles, (0, 2, 3, 1, 4)).reshape(
        NVT, pair_rows * rows_local, row_most * TILE
    )
    int_ids = int_table[second_lists[:, :, None], second_lists[:, None, :]]
    both_found = found_lists[:, :, None] & found_lists[:, None, :]
    int_ids = jnp.where(both_found, int_ids, int_count)
    right_tiles = int_pad[int_ids].reshape(NVT, row_most, row_most, TILE, TILE)
    right_matrix = jnp.transpose(right_tiles, (0, 2, 4, 1, 3)).reshape(
        NVT, row_most * TILE, row_most * TILE
    )
    product = jnp.einsum(
        "rmx,rxy->rmy", left_matrix, right_matrix, preferred_element_type=jnp.float32
    )
    product = product.astype(jnp.bfloat16).reshape(NVT, pair_rows, rows_local, row_most, TILE)
    dressed_flat = jnp.transpose(product, (0, 3, 1, 2, 4)).reshape(
        NVT * row_most, pair_rows, row_cells
    )
    dressed_flat = jnp.concatenate(
        [dressed_flat, jnp.zeros((1, pair_rows, row_cells), dressed_flat.dtype)], axis=0
    )
    row_tile = amp_tiles // NVT
    col_tile = amp_tiles % NVT
    flat_ids = row_tile * row_most + place[row_tile, col_tile]
    flat_pad = jnp.concatenate([flat_ids, jnp.array([NVT * row_most], dtype=jnp.int32)])
    chosen = dressed_flat[flat_pad[slot_ids]]
    send_dressed = jnp.transpose(chosen, (1, 0, 2)).reshape(pair_rows, wide_size, CAP, row_cells)
    amp_part = lax.all_to_all(send_amps, "wide", split_axis=1, concat_axis=0, tiled=True)
    dress_part = lax.all_to_all(send_dressed, "wide", split_axis=1, concat_axis=0, tiled=True)
    ladder_part = jnp.einsum(
        "pq,qucr->pucr", hole_ladder, amp_part, preferred_element_type=jnp.float32
    )
    combined = (ladder_part + dress_part.astype(jnp.float32)).astype(jnp.bfloat16)
    return combined.reshape(pair_rows * wide_size, CAP, row_cells)


def solution(mesh):
    return jax.shard_map(
        per_device,
        mesh=mesh,
        in_specs=(P("wide", None, "narrow"), P("narrow", None), P(), P(), P(), P()),
        out_specs=P(None, "wide", "narrow"),
        check_vma=False,
    )
```

profile of v0, /device:TPU:1, one launch (start us, length us, event | category | flops | bytes accessed | tf_op | source)
XLA Modules:
  0.0 225.0 jit_solution(10802741785969215572)
XLA Ops:
  11.9 6.0 %gather_fusion.2 = s32[864]{0:T(1024)S(1)} fusion(s32[24,24]{1,0:T(8,128)S(1)} %select_n.166, s32[864]{0:T(1024)S(1)} %reshape.203), kind=kCustom, calls=%fused_computation.2 | custom fusion | bytes 13824 | tf_op jit(solution)/shard_map/gather | solution.py:67
  19.2 1.1 gather_fusion.1
  20.9 0.9 copy.53
  21.8 1.0 reshape.179
  22.8 1.3 gather_fusion.4
  24.6 1.9 gather_fusion.5
  26.6 27.8 %all-gather.2.cloned.1.call-done = bf16[192,4096]{1,0:T(8,128)(2,1)} async-done(((bf16[24,4096]{1,0:T(8,128)(2,1)}), bf16[192,4096]{1,0:T(8,128)(2,1)}) %all-gather.2.cloned.1.call-update) | async-done | bytes 1572880 | tf_op jit(solution)/shard_map/all_gather | solution.py:57
  54.4 1.6 concatenate.19
  56.0 6.5 %gather_fusion.3 = bf16[864,4096]{1,0:T(8,128)(2,1)} fusion(bf16[193,4096]{1,0:T(8,128)(2,1)S(1)} %concatenate.19, s32[1024]{0:T(1024)S(1)} %pad_clamp_fusion.1), kind=kCustom, calls=%fused_computation.3 | custom fusion | bytes 14159232 | tf_op jit(solution)/shard_map/gather | solution.py:70
  62.5 20.0 %reshape.180 = bf16[24,6,6,64,64]{4,3,2,1,0:T(8,128)(2,1)} reshape(bf16[864,4096]{1,0:T(8,128)(2,1)} %gather_fusion.3) | data formatting | bytes 14155776 | tf_op jit(solution)/shard_map/reshape | solution.py:70
  82.5 22.5 %copy.41 = bf16[24,6,6,64,64]{3,1,4,2,0:T(8,128)(2,1)} copy(bf16[24,6,6,64,64]{4,3,2,1,0:T(8,128)(2,1)} %reshape.180) | data formatting | bytes 14155776 | tf_op jit(solution)/shard_map/reshape | solution.py:70
  105.0 23.4 %reshape.181 = bf16[24,384,384]{2,1,0:T(8,128)(2,1)} reshape(bf16[24,6,64,6,64]{4,3,2,1,0:T(8,128)(2,1)} %bitcast.50) | data formatting | bytes 14155776 | tf_op jit(solution)/shard_map/reshape | solution.py:71
  128.4 4.2 %convolution_convert_fusion = bf16[24,32,384]{2,1,0:T(8,128)(2,1)S(1)} fusion(bf16[24,32,384]{2,1,0:T(8,128)(2,1)S(1)} %reshape.179, bf16[24,384,384]{2,1,0:T(8,128)(2,1)} %reshape.181), kind=kOutput, calls=%fused_computation.11 | convolution fusion | flops 226787328 | bytes 8257536 | tf_op jit(solution)/shard_map/rmx,rxy->rmy/dot_general | solution.py:74
  134.6 2.4 %gather_fusion.6 = bf16[256,4,512]{2,1,0:T(4,128)(2,1)} fusion(bf16[145,4,512]{2,1,0:T(4,128)(2,1)S(1)} %concatenate.21, s32[1024]{0:T(1024)S(1)} %pad_clamp_fusion), kind=kCustom, calls=%fused_computation.6 | custom fusion | bytes 2098176 | tf_op jit(solution)/shard_map/gather | solution.py:88
  137.0 14.4 %all-to-all-start.1 = ((bf16[4,64,4,512]{3,0,2,1:T(4,128)(2,1)}), bf16[4,64,4,512]{3,0,2,1:T(4,128)(2,1)S(1)}, u32[]{:S(2)}, u32[]{:S(2)}) async-start(bf16[4,64,4,512]{3,0,2,1:T(4,128)(2,1)} %bitcast.18), calls=%async_computation.1 | async-start | bytes 2097152 | tf_op jit(solution)/shard_map/all_to_all | solution.py:91
  151.5 1.5 gather_fusion
  153.0 1.5 copy.33
  154.5 24.9 %all-to-all-done.1 = bf16[4,64,4,512]{3,0,2,1:T(4,128)(2,1)S(1)} async-done(((bf16[4,64,4,512]{3,0,2,1:T(4,128)(2,1)}), bf16[4,64,4,512]{3,0,2,1:T(4,128)(2,1)S(1)}, u32[]{:S(2)}, u32[]{:S(2)}) %all-to-all-start.1) | async-done | bytes 1048608 | tf_op jit(solution)/shard_map/all_to_all | solution.py:91
  179.5 6.5 %all-to-all-start = ((bf16[4,64,4,512]{3,2,0,1:T(4,128)(2,1)}), bf16[4,64,4,512]{3,2,0,1:T(4,128)(2,1)S(1)}, u32[]{:S(2)}, u32[]{:S(2)}) async-start(bf16[4,64,4,512]{3,2,0,1:T(4,128)(2,1)} %copy.33), calls=%async_computation | async-start | bytes 2097152 | tf_op jit(solution)/shard_map/all_to_all | solution.py:90
  186.3 2.3 %copy.44 = f32[64,4,1,4,512]{4,3,1,0,2:T(4,128)} copy(f32[64,4,1,4,512]{4,1,3,0,2:T(4,128)S(1)} %convert_bitcast_fusion) | data formatting | bytes 4194304 | tf_op jit(solution)/shard_map/convert_element_type | solution.py:95
  188.6 1.9 copy.45
  190.5 23.4 %all-to-all-done = bf16[4,64,4,512]{3,2,0,1:T(4,128)(2,1)S(1)} async-done(((bf16[4,64,4,512]{3,2,0,1:T(4,128)(2,1)}), bf16[4,64,4,512]{3,2,0,1:T(4,128)(2,1)S(1)}, u32[]{:S(2)}, u32[]{:S(2)}) %all-to-all-start) | async-done | bytes 1048608 | tf_op jit(solution)/shard_map/all_to_all | solution.py:90
  213.9 1.6 fusion
  215.5 2.6 %copy.46 = bf16[256,4,512]{2,1,0:T(4,128)(2,1)} copy(bf16[256,4,512]{0,2,1:T(8,128)(2,1)} %fusion) | data formatting | bytes 2097152 | tf_op jit(solution)/shard_map/convert_element_type | solution.py:95
  (57 shorter events, 9.9 us)
Async XLA Ops:
  6.5 207.4 %copy-start = (bf16[256,256]{1,0:T(8,128)(2,1)S(1)}, bf16[256,256]{1,0:T(8,128)(2,1)}, u32[]{:S(2)}) copy-start(bf16[256,256]{1,0:T(8,128)(2,1)} %param.9) | copy-start | bytes 393220
  6.5 47.9 %all-gather.2.cloned.1.call-start = ((), (), s32[]{:S(2)}) async-start(), calls=%async_computation.2 | async-start | bytes 1769472 | tf_op jit(solution)/shard_map/all_gather | solution.py:57
  11.8 6.7 %copy-start.1 = (bf16[4,128,512]{2,1,0:T(8,128)(2,1)S(1)}, bf16[4,128,512]{2,1,0:T(8,128)(2,1)}, u32[]{:S(2)}) copy-start(bf16[4,128,512]{2,1,0:T(8,128)(2,1)} %param.7) | copy-start | bytes 1572868
  20.8 2.0 copy-start.2
  20.8 3.3 %copy-start.3 = (s32[128,1]{0,1:T(1,128)S(1)}, s32[128,1]{0,1:T(1,128)}, u32[]{:S(2)}) copy-start(s32[128,1]{0,1:T(1,128)} %param.12) | copy-start | bytes 1540
  137.0 42.4 %all-to-all-start.1 = ((bf16[4,64,4,512]{3,0,2,1:T(4,128)(2,1)}), bf16[4,64,4,512]{3,0,2,1:T(4,128)(2,1)S(1)}, u32[]{:S(2)}, u32[]{:S(2)}) async-start(bf16[4,64,4,512]{3,0,2,1:T(4,128)(2,1)} %bitcast.18), calls=%async_computation.1 | async-start | bytes 2097152 | tf_op jit(solution)/shard_map/all_to_all | solution.py:91
  179.5 34.5 %all-to-all-start = ((bf16[4,64,4,512]{3,2,0,1:T(4,128)(2,1)}), bf16[4,64,4,512]{3,2,0,1:T(4,128)(2,1)S(1)}, u32[]{:S(2)}, u32[]{:S(2)}) async-start(bf16[4,64,4,512]{3,2,0,1:T(4,128)(2,1)} %copy.33), calls=%async_computation | async-start | bytes 2097152 | tf_op jit(solution)/shard_map/all_to_all | solution.py:90
Sparse Core Ops, SparseCore 0:
  9.4 44.9 all-gather.1
where the time goes:
time: 227 us; the launch traced here: 225 us
  local copies, waits for them, and re-layouts  103 us (45%)
  waiting for transfers between devices  76.9 us (34%)
  starting transfers between devices  20.9 us (9%)
  between operations  13.8 us (6%)
  matrix products  5.73 us (3%)
  other arithmetic  4.96 us (2%)
    reshape x2, local copies, waits for them, and re-layouts, per_device(): right_tiles = int_pad[int_ids].reshape(NVT, row_most, row_most, TILE, TILE)  42.5 us
    all_gather x1, waiting for transfers between devices, per_device(): int_all = lax.all_gather(int_values, 'narrow', axis=0, tiled=True)  27.8 us
    all_to_all x1, waiting for transfers between devices, per_device(): lax.all_to_all(send_dressed, 'wide', split_axis=1, concat_axis=0, tiled=T...  24.9 us
    all_to_all x1, waiting for transfers between devices, per_device(): lax.all_to_all(send_amps, 'wide', split_axis=1, concat_axis=0, tiled=True)  23.4 us
    reshape x1, local copies, waits for them, and re-layouts, per_device(): jnp.transpose(right_tiles, (0, 2, 4, 1, 3))  23.4 us
    all_to_all x1, starting transfers between devices, per_device(): lax.all_to_all(send_dressed, 'wide', split_axis=1, concat_axis=0, tiled=T...  14.4 us
    gather x1, local copies, waits for them, and re-layouts, per_device(): right_tiles = int_pad[int_ids].reshape(NVT, row_most, row_most, TILE, TILE)  6.55 us
    all_to_all x1, starting transfers between devices, per_device(): lax.all_to_all(send_amps, 'wide', split_axis=1, concat_axis=0, tiled=True)  6.46 us
  transfers between devices with their start and end apart: 3, of which 3 were waited for; matrix products, arithmetic and copies ran while one was open for 12% of the time, Pallas kernels for 0%

commit v1 on v0

v1 whole, which is shorter than its diff:
```python
import functools

import jax
import jax.numpy as jnp
from jax import lax
from jax.experimental import pallas as pl
from jax.experimental.pallas import tpu as pltpu
from jax.sharding import PartitionSpec as P

TILE = 64
NVT = 24
CAP = 4
MESH = pl.DeviceIdType.MESH
NT = (((1,), (1,)), ((), ()))
BF16, F32, I32 = jnp.bfloat16, jnp.float32, jnp.int32


def iota(shape, dim):
    return lax.broadcasted_iota(I32, shape, dim)


def hot(mask):
    return jnp.where(mask, 1.0, 0.0).astype(BF16)


def mm(a, b):
    return jnp.dot(a, b, preferred_element_type=F32)


def column_of(row):
    n = row.shape[1]
    eye = iota((n, n), 0) == iota((n, n), 1)
    return jnp.sum(jnp.where(eye, row, 0), axis=1, keepdims=True)


def kernel(wn, zn, table_ref, amp_ref, int_ref, hole_ref, codes_ref, owner_ref, out_ref,
           gath, tiles, idense, adense, zbuf, dress, pick, send_a, send_d, recv_a, recv_d, hexp, acc,
           z_send, z_recv, c_send, c_recv, a_send, a_recv, d_send, d_recv):
    wide = lax.axis_index("wide")
    narrow = lax.axis_index("narrow")
    core = lax.rem(wide, 2)
    other = wide + 1 - 2 * core
    cells = amp_ref.shape[1]
    blocks = cells // 128
    pairs = hole_ref.shape[0] // wn
    kt = amp_ref.shape[0] // pairs
    rows = CAP * pairs
    ki = tiles.shape[0] - 1
    share = ki // zn
    half_rows = share * 16
    cells_all = NVT * NVT
    low = iota((1, 128), 1) < TILE

    barrier = pltpu.get_barrier_semaphore()
    ring = sorted({1, zn - 1})

    def greet(i, c):
        pl.semaphore_signal(barrier, inc=1, device_id=(lax.rem(wide + i, wn), narrow), device_id_type=MESH)
        return c

    for step in ring:
        pl.semaphore_signal(barrier, inc=1, device_id=(wide, lax.rem(narrow + step, zn)), device_id_type=MESH)
    lax.fori_loop(1, wn, greet, 0)

    owner_row = owner_ref[...]
    owner_col = column_of(owner_row)
    before = iota((kt, kt), 0) < iota((kt, kt), 1)
    count = jnp.sum(jnp.where(before & (owner_col == owner_row), 1, 0), axis=0, keepdims=True)
    place = (owner_row * CAP + count) * pairs
    place = jnp.concatenate([place + p for p in range(pairs)], axis=1)
    pick[...] = hot(iota((wn * rows, pairs * kt), 0) == place)

    pl.semaphore_wait(barrier, wn - 1 + len(ring))

    right_hops, left_hops = zn // 2, (zn - 1) // 2

    def half(ref, shard, who):
        return ref.at[shard, pl.ds(pl.multiple_of(who * half_rows, 16), half_rows)]

    def hop(way, step, do):
        sign = 1 if way == 0 else zn - 1
        shard = lax.rem(narrow + (zn - sign) * (step - 1), zn)
        src = half(gath, shard, core) if step > 1 else int_ref.at[
            pl.ds(pl.multiple_of(core * half_rows, 16), half_rows)]
        k = step - 1 if way == 0 else right_hops + step - 1
        copy = pltpu.make_async_remote_copy(
            src_ref=src, dst_ref=half(gath, shard, core), send_sem=z_send.at[k], recv_sem=z_recv.at[k],
            device_id=(wide, lax.rem(narrow + sign, zn)), device_id_type=MESH)
        do(copy)

    def hand(way, step, do):
        sign = 1 if way == 0 else zn - 1
        shard = lax.rem(narrow + (zn - sign) * step, zn)
        k = step - 1 if way == 0 else right_hops + step - 1
        copy = pltpu.make_async_remote_copy(
            src_ref=half(gath, shard, core), dst_ref=half(gath, shard, core), send_sem=c_send.at[k],
            recv_sem=c_recv.at[k], device_id=(other, narrow), device_id_type=MESH)
        do(copy)

    def spread(block, first):
        n = block.shape[0] // 32
        x = block.astype(F32)
        y = pltpu.roll(x, TILE, 1)
        even = jnp.where(low, x, y).astype(BF16).reshape(n, 32, 128)
        odd = jnp.where(low, y, x).astype(BF16).reshape(n, 32, 128)
        tiles[pl.ds(first, n), pl.ds(0, 32)] = even
        tiles[pl.ds(first, n), pl.ds(32, 32)] = odd

    def spread_half(way, step, who):
        sign = 1 if way == 0 else zn - 1
        shard = lax.rem(narrow + (zn - sign) * step, zn)
        spread(half(gath, shard, who)[...], shard * share + who * (share // 2))

    hops = [(w, s) for s in range(1, right_hops + 1) for w in (0, 1) if s <= (right_hops, left_hops)[w]]
    start = lambda copy: copy.start()
    for w, s in hops:
        if s == 1:
            hop(w, s, start)

    def post(send, recv, s_sem, r_sem, do):
        def one(i, c):
            i = lax.rem(i + 3 * wn // 8, wn - 1) + 1
            to = lax.rem(wide + i, wn)
            copy = pltpu.make_async_remote_copy(
                src_ref=send.at[pl.ds(pl.multiple_of(to * rows, 16), rows)],
                dst_ref=recv.at[pl.ds(pl.multiple_of(wide * rows, 16), rows)],
                send_sem=s_sem.at[i], recv_sem=r_sem.at[i], device_id=(to, narrow), device_id_type=MESH)
            do(copy)
            return c
        lax.fori_loop(0, wn - 1, one, 0)

    send_a[...] = mm(pick[...], amp_ref[...]).astype(BF16)
    post(send_a, recv_a, a_send, a_recv, start)
    mine = pl.ds(pl.multiple_of(wide * rows, 16), rows)
    recv_a[mine] = send_a[mine]

    tiles[ki] = jnp.zeros((TILE, 128), BF16)
    spread(int_ref[...], narrow * share)

    codes = codes_ref[...]
    second = lax.rem(codes, NVT)
    cell = lax.rem(second, 2) * (cells_all // 2) + lax.div(second, 2) * NVT + lax.div(codes, NVT)
    onto = hot(iota((cells_all, kt), 0) == cell)

    def dense_pair(p):
        g = mm(onto, amp_ref[pl.ds(p * kt, kt), :])
        hf = cells_all // 2
        for m in range(blocks):
            ge, go = g[:hf, m * 128:(m + 1) * 128], g[hf:, m * 128:(m + 1) * 128]
            y0 = jnp.where(low, ge, pltpu.roll(go, TILE, 1))
            y1 = jnp.where(low, pltpu.roll(ge, TILE, 1), go)
            for h in range(NVT // 2):
                both = jnp.concatenate([y0[h * NVT:(h + 1) * NVT], y1[h * NVT:(h + 1) * NVT]], axis=0)
                adense[pl.ds((p * blocks + m) * 2 * NVT, 2 * NVT), pl.ds(h * 128, 128)] = both.astype(BF16)

    rounds = [[(w, s) for w, s in hops if s == r] for r in range(1, right_hops + 1)]
    todo = list(range(pairs))
    for r, ready in enumerate(rounds):
        if todo:
            dense_pair(todo.pop(0))
        for w, s in ready:
            hop(w, s, lambda copy: copy.wait_recv())
            hand(w, s, start)
            if (w, s + 1) in hops:
                hop(w, s + 1, start)
        for w, s in ready:
            spread_half(w, s, core)
    for p in todo:
        dense_pair(p)
    for w, s in hops:
        hand(w, s, lambda copy: copy.wait_recv())
        spread_half(w, s, 1 - core)

    def gather_row(c, carry):
        for h in range(NVT // 2):
            left = tiles[table_ref[c * NVT + 2 * h]]
            right = tiles[table_ref[c * NVT + 2 * h + 1]]
            idense[pl.ds(pl.multiple_of(c * TILE, TILE), TILE), pl.ds(h * 128, 128)] = jnp.where(low, left, right)
        return carry

    lax.fori_loop(0, NVT, gather_row, 0)

    def product(n, carry):
        rhs = idense[pl.ds(pl.multiple_of(n * 256, 256), 256), :]
        d = lax.dot_general(adense[...], rhs, NT, preferred_element_type=F32)
        for p in range(pairs):
            for m in range(blocks):
                at = (p * blocks + m) * 2 * NVT
                z0, z1 = [], []
                for j in range(2):
                    x0 = d[at:at + NVT, j * 128:(j + 1) * 128]
                    x1 = d[at + NVT:at + 2 * NVT, j * 128:(j + 1) * 128]
                    z0.append(jnp.where(low, x0, pltpu.roll(x1, TILE, 1)))
                    z1.append(jnp.where(low, pltpu.roll(x0, TILE, 1), x1))
                to = pl.multiple_of(n * 2 * NVT, 16)
                zbuf[p, pl.ds(to, 2 * NVT), pl.ds(m * 128, 128)] = jnp.concatenate(z0, axis=0).astype(BF16)
                zbuf[p, pl.ds(to + cells_all // 2, 2 * NVT), pl.ds(m * 128, 128)] = jnp.concatenate(
                    z1, axis=0).astype(BF16)
        return carry

    lax.fori_loop(0, NVT // 4, product, 0)

    off = iota((kt, cells_all), 1) == column_of(cell)
    take = hot(off)
    u, v = iota((128, 128), 0), iota((128, 128), 1)
    back = hot(v == (u & 64) + (u & 31) * 2 + ((u >> 5) & 1))
    for p in range(pairs):
        got = mm(take, zbuf[p]).astype(BF16)
        for m in range(blocks):
            dress[pl.ds(p * kt, kt), pl.ds(m * 128, 128)] = mm(got[:, m * 128:(m + 1) * 128], back).astype(BF16)
    send_d[...] = mm(pick[...], dress[...]).astype(BF16)
    post(send_d, recv_d, d_send, d_recv, start)
    recv_d[mine] = send_d[mine]

    total = wn * rows
    np_all = hole_ref.shape[0]
    r0, c0 = iota((total, np_all), 0), iota((total, np_all), 1)
    by_row = mm(hot(lax.div(r0, CAP) == c0), hole_ref[...]).astype(BF16)
    r1, c1 = iota((np_all, total), 0), iota((np_all, total), 1)
    spread_cols = hot(lax.div(c1, rows) * pairs + lax.rem(c1, pairs) == r1)
    chunk = 8 * rows if wn % 8 == 0 else total
    r2, c2 = iota((chunk, total), 0), iota((chunk, total), 1)
    same = lax.rem(r2, CAP) == lax.rem(lax.div(c2, pairs), CAP)
    for y in range(total // chunk):
        hexp[pl.ds(y * chunk, chunk), :] = jnp.where(
            same, mm(by_row[y * chunk:(y + 1) * chunk], spread_cols), 0.0).astype(BF16)

    post(send_a, recv_a, a_send, a_recv, lambda copy: copy.wait_recv())

    def ladder(y, carry):
        at = pl.ds(pl.multiple_of(y * chunk, 16), chunk)
        acc[at, :] = mm(hexp[at, :], recv_a[...])
        return carry

    lax.fori_loop(0, total // chunk, ladder, 0)

    post(send_d, recv_d, d_send, d_recv, lambda copy: copy.wait_recv())
    r3, c3 = iota((chunk, chunk), 0), iota((chunk, chunk), 1)
    want = lax.div(r3, rows) * rows + lax.rem(r3, CAP) * pairs + lax.rem(lax.div(r3, CAP), pairs)
    turn = hot(c3 == want)

    def finish(y, carry):
        at = pl.ds(pl.multiple_of(y * chunk, 16), chunk)
        out_ref[at, :] = (acc[at, :] + mm(turn, recv_d[at, :])).astype(BF16)
        return carry

    lax.fori_loop(0, total // chunk, finish, 0)

    for w, s in hops:
        hop(w, s, lambda copy: copy.wait_send())
        hand(w, s, lambda copy: copy.wait_send())
    post(send_a, recv_a, a_send, a_recv, lambda copy: copy.wait_send())
    post(send_d, recv_d, d_send, d_recv, lambda copy: copy.wait_send())


def per_device(wn, zn, amplitudes, int_values, hole_ladder, amp_tiles, int_tiles, owner):
    pairs, kt, cells = amplitudes.shape
    share = int_values.shape[0]
    ki = share * zn
    rows = CAP * pairs
    total = wn * rows
    blocks = cells // 128
    matches = jnp.arange(NVT * NVT, dtype=I32)[:, None] == int_tiles[None, :]
    table = ki + jnp.sum(jnp.where(matches, jnp.arange(ki, dtype=I32)[None, :] - ki, 0), axis=1)
    hops = zn - 1
    vmem = pl.BlockSpec(memory_space=pltpu.VMEM)
    out = pl.pallas_call(
        functools.partial(kernel, wn, zn),
        out_shape=jax.ShapeDtypeStruct((total, cells), BF16),
        in_specs=[pl.BlockSpec(memory_space=pltpu.SMEM)] + [vmem] * 5,
        out_specs=vmem,
        scratch_shapes=[
            pltpu.VMEM((zn, share * 32, 128), BF16),
            pltpu.VMEM((ki + 1, TILE, 128), BF16),
            pltpu.VMEM((NVT * TILE, NVT * TILE), BF16),
            pltpu.VMEM((pairs * blocks * 2 * NVT, NVT * TILE), BF16),
            pltpu.VMEM((pairs, NVT * NVT, cells), BF16),
            pltpu.VMEM((pairs * kt, cells), BF16),
            pltpu.VMEM((total, pairs * kt), BF16),
            pltpu.VMEM((total, cells), BF16),
            pltpu.VMEM((total, cells), BF16),
            pltpu.VMEM((total, cells), BF16),
            pltpu.VMEM((total, cells), BF16),
            pltpu.VMEM((total, total), BF16),
            pltpu.VMEM((total, cells), F32),
            pltpu.SemaphoreType.DMA((hops,)),
            pltpu.SemaphoreType.DMA((hops,)),
            pltpu.SemaphoreType.DMA((hops,)),
            pltpu.SemaphoreType.DMA((hops,)),
            pltpu.SemaphoreType.DMA((wn,)),
            pltpu.SemaphoreType.DMA((wn,)),
            pltpu.SemaphoreType.DMA((wn,)),
            pltpu.SemaphoreType.DMA((wn,)),
        ],
        compiler_params=pltpu.CompilerParams(
            collective_id=0, has_side_effects=True, vmem_limit_bytes=58 * 1024 * 1024
        ),
        cost_estimate=pl.CostEstimate(flops=8 * 10**9, bytes_accessed=4 * 10**6, transcendentals=0),
    )(
        table,
        amplitudes.reshape(pairs * kt, cells),
        int_values.reshape(share * 32, 128),
        hole_ladder,
        amp_tiles.reshape(1, kt),
        owner.reshape(1, kt),
    )
    return out.reshape(wn * pairs, CAP, cells)


def solution(mesh):
    wn, zn = mesh.shape["wide"], mesh.shape["narrow"]
    return jax.shard_map(
        functools.partial(per_device, wn, zn),
        mesh=mesh,
        in_specs=(P("wide", None, "narrow"), P("narrow", None), P(), P(), P(), P()),
        out_specs=P(None, "wide", "narrow"),
        check_vma=False,
    )
```

time: 227 us -> 80.4 us (0.35)
  local copies, waits for them, and re-layouts: 103 us -> 4.51 us
  waiting for transfers between devices: 76.9 us -> 0 us
  Pallas kernels: 0 us -> 74.4 us
  starting transfers between devices: 20.9 us -> 0 us
  between operations: 13.8 us -> 0.02 us
  matrix products: 5.73 us -> 0 us
  other arithmetic: 4.96 us -> 0.72 us
    pallas_call x0 -> x1, Pallas kernels: none -> 74.4 us  [per_device(): pl.pallas_call(functools.partial(kernel, wn, zn), out_shape=jax.ShapeDtyp...]
    reshape x10 -> x2, local copies, waits for them, and re-layouts: 71.7 us -> 3.83 us  [the longest x1 2.14 us: per_device(): return out.reshape(wn * pairs, CAP, cells)]
    all_to_all x2 -> x0, waiting for transfers between devices: 48.3 us -> none  [the longest x1 24.9 us: per_device(): lax.all_to_all(send_dressed, 'wide', split_axis=1, concat_axis=0, tiled=T...]
    all_gather x1 -> x0, waiting for transfers between devices: 27.8 us -> none  [per_device(): int_all = lax.all_gather(int_values, 'narrow', axis=0, tiled=True)]
    gather x8 -> x0, local copies, waits for them, and re-layouts: 20.9 us -> none  [the longest x1 6.55 us: per_device(): right_tiles = int_pad[int_ids].reshape(NVT, row_most, row_most, TILE, TILE)]
    all_to_all x2 -> x0, starting transfers between devices: 20.9 us -> none  [the longest x1 14.4 us: per_device(): lax.all_to_all(send_dressed, 'wide', split_axis=1, concat_axis=0, tiled=T...]
    convert_element_type x3 -> x0, local copies, waits for them, and re-layouts: 6.87 us -> none  [the longest x2 4.24 us: per_device(): dress_part.astype(jnp.float32)]
    dot_general x2 -> x0, matrix products: 5.73 us -> none  [the longest x1 4.15 us: per_device(): jnp.einsum('rmx,rxy->rmy', left_matrix, right_matrix, preferred_element_t...]
  transfers between devices with their start and end apart: 3 -> 0, of which waited for: 3 -> 0; matrix products, arithmetic and copies ran while one was open for 12% -> 0% of each run, Pallas kernels for 0% -> 0%
where the time goes in v1:
time: 80.4 us; the launch traced here: 79.6 us
  Pallas kernels  74.4 us (93%)
  local copies, waits for them, and re-layouts  4.51 us (6%)
    pallas_call x1, Pallas kernels, per_device(): pl.pallas_call(functools.partial(kernel, wn, zn), out_shape=jax.ShapeDtyp...  74.4 us
    reshape x1, local copies, waits for them, and re-layouts, per_device(): return out.reshape(wn * pairs, CAP, cells)  2.14 us
    reshape x1, local copies, waits for them, and re-layouts, per_device(): int_values.reshape(share * 32, 128)  1.7 us

profile of v1, /device:TPU:1, one launch (start us, length us, event | category | flops | bytes accessed | tf_op | source)
XLA Modules:
  0.0 79.6 jit_solution(7459844397197698861)
XLA Ops:
  0.0 0.0 copy-start
  0.0 0.7 copy-done
  0.7 0.1 select_reduce_fusion
  0.8 0.6 broadcast_add_fusion.table_ref
  1.4 1.7 %reshape.22.int_ref = bf16[768,128]{1,0:T(8,128)(2,1)} reshape(bf16[24,4096]{1,0:T(8,128)(2,1)} %param.7) | data formatting | bytes 393216 | tf_op jit(solution)/shard_map/reshape | solution.py:302
  3.1 74.4 %shard_map.64 = bf16[1024,512]{1,0:T(8,128)(2,1)} custom-call(s32[576]{0:T(1024)} %broadcast_add_fusion.table_ref, bf16[512,512]{1,0:T(8,128)(2,1)} %bitcast.3, bf16[768,128]{1,0:T(8,128)(2,1)} %reshape.22.int_ref, bf16[256,256]{1,0:T(8,128)(2,1)} %hole_ref.1, s32[1,128]{1,0:T(1,128)} %bitcast.4, s32[1,128]{1,0:T(1,128)} %bitcast.5), custom_call_target="tpu_custom_call" | custom-call | flops 8000000000 | bytes 4000000 | tf_op jit(solution)/shard_map/pallas_call | solution.py:267
  77.5 2.1 %reshape.25 = bf16[256,4,512]{2,1,0:T(4,128)(2,1)} reshape(bf16[1024,512]{1,0:T(8,128)(2,1)} %shard_map.64) | data formatting | bytes 2097152 | tf_op jit(solution)/shard_map/reshape | solution.py:307
  (1 shorter events, 0.0 us)
Async XLA Ops:
  0.0 0.7 copy-start

commit v2 on v0

v2 whole, which is shorter than its diff:
```python
import functools

import jax
import jax.numpy as jnp
from jax import lax
from jax.experimental import pallas as pl
from jax.experimental.pallas import tpu as pltpu
from jax.sharding import PartitionSpec as P

TILE = 64
NVT = 24
CAP = 4
ROW = 8
ROOMS = (20, 24, 32)
MESH = pl.DeviceIdType.MESH
NT = (((1,), (1,)), ((), ()))
BF16, F32, I32 = jnp.bfloat16, jnp.float32, jnp.int32


def iota(shape, dim):
    return lax.broadcasted_iota(I32, shape, dim)


def hot(mask):
    return jnp.where(mask, 1.0, 0.0).astype(BF16)


def mm(a, b):
    return jnp.dot(a, b, preferred_element_type=F32)


def column_of(row):
    n = row.shape[1]
    eye = iota((n, n), 0) == iota((n, n), 1)
    return jnp.sum(jnp.where(eye, row, 0), axis=1, keepdims=True)


def far_first(n):
    return sorted(range(1, n), key=lambda d: (-min(d, n - d), d))


def begin(copy):
    copy.start()


def landed(copy):
    copy.wait_recv()


def left(copy):
    copy.wait_send()


def kernel(wn, zn, room, table_ref, amp_ref, int_ref, hole_ref, codes_ref, owner_ref, out_ref,
           local, local32, gath, tiles, idense, adense, zbuf, dress, pick, pack_a, pack_d, leg_a, leg_d,
           turn_a, turn_d, recv_a, recv_d, hexp, acc,
           z_send, z_recv, x_send, x_recv, c_send, c_recv,
           ya_send, ya_recv, yd_send, yd_recv, ra_send, ra_recv, rd_send, rd_recv):
    wide = lax.axis_index("wide")
    narrow = lax.axis_index("narrow")
    yn = wn // ROW
    y = lax.div(wide, ROW)
    g = lax.rem(wide, ROW)
    other = wide + 1 - 2 * lax.rem(wide, 2)
    cells = amp_ref.shape[1]
    blocks = cells // 128
    pairs = hole_ref.shape[0] // wn
    kt = amp_ref.shape[0] // pairs
    rows = CAP * pairs
    row_rows = ROW * rows
    parcel = room * pairs
    ki = tiles.shape[0] - 1
    share = ki // zn
    sub = share // ROW
    cells_all = NVT * NVT
    hf = cells_all // 2
    low = iota((1, 128), 1) < TILE
    y_order, z_order = far_first(yn), far_first(zn)
    mates = range(2, ROW, 2)

    def at_y(step):
        return (lax.rem(y + step, yn) * ROW + g, narrow)

    def at_g(step):
        return (y * ROW + lax.rem(g + step, ROW), narrow)

    def at_z(step):
        return (wide, lax.rem(narrow + step, zn))

    barrier = pltpu.get_barrier_semaphore()
    peers = [at_z(s) for s in z_order] + [at_y(s) for s in y_order] + [at_g(s) for s in range(1, ROW)]
    for peer in peers:
        pl.semaphore_signal(barrier, inc=1, device_id=peer, device_id_type=MESH)

    own = int_ref[...].astype(F32)
    for m in range(32):
        local32[pl.ds(m, share, stride=32), :] = own[:, m * 128:(m + 1) * 128]
    local[...] = local32[...].astype(BF16)

    owner_row = owner_ref[...]
    owner_col = column_of(owner_row)
    before = iota((kt, kt), 0) < iota((kt, kt), 1)
    count = jnp.sum(jnp.where(before & (owner_col == owner_row), 1, 0), axis=0, keepdims=True)
    slot = owner_row * CAP + count
    line = lax.div(owner_row, ROW)
    rank = jnp.sum(jnp.where(before & (lax.div(owner_col, ROW) == line), 1, 0), axis=0, keepdims=True)
    key = line * room + rank
    slot = jnp.concatenate([slot * pairs + p for p in range(pairs)], axis=1)
    key = jnp.concatenate([key * pairs + p for p in range(pairs)], axis=1)
    pick[...] = hot(iota((yn * parcel, pairs * kt), 0) == key)

    pl.semaphore_wait(barrier, len(peers))

    def part(shard, who):
        return pl.ds(pl.multiple_of((shard * share + who * sub) * 32, 16), sub * 32)

    def z_copy(step):
        return pltpu.make_async_remote_copy(
            src_ref=local.at[pl.ds(pl.multiple_of(g * sub * 32, 16), sub * 32)], dst_ref=gath.at[part(narrow, g)],
            send_sem=z_send.at[step], recv_sem=z_recv.at[step], device_id=at_z(step), device_id_type=MESH)

    def from_z(step):
        return lax.rem(narrow + zn - step, zn)

    def x_copy(step, e):
        at = gath.at[part(from_z(step), g)]
        k = step * ROW + e
        return pltpu.make_async_remote_copy(
            src_ref=at, dst_ref=at, send_sem=x_send.at[k], recv_sem=x_recv.at[k], device_id=at_g(e),
            device_id_type=MESH)

    def c_copy(step, e):
        at = gath.at[part(from_z(step), lax.rem(g + ROW - e, ROW))]
        k = step * ROW + e
        return pltpu.make_async_remote_copy(
            src_ref=at, dst_ref=at, send_sem=c_send.at[k], recv_sem=c_recv.at[k], device_id=(other, narrow),
            device_id_type=MESH)

    def spread(block, first):
        n = block.shape[0] // 32
        turned = pltpu.roll(block, TILE, 1)
        tiles[pl.ds(first, n), pl.ds(0, 32)] = jnp.where(low, block, turned).reshape(n, 32, 128)
        tiles[pl.ds(first, n), pl.ds(32, 32)] = jnp.where(low, turned, block).reshape(n, 32, 128)

    def y_copy(pack, leg, s_sem, r_sem, step):
        to = lax.rem(y + step, yn)
        return pltpu.make_async_remote_copy(
            src_ref=pack.at[pl.ds(pl.multiple_of(to * parcel, 16), parcel)],
            dst_ref=leg.at[pl.ds(step * parcel, parcel)],
            send_sem=s_sem.at[step], recv_sem=r_sem.at[step], device_id=at_y(step), device_id_type=MESH)

    def from_y(step):
        return lax.rem(y + yn - step, yn)

    def r_each(turned, recv, s_sem, r_sem, step, do):
        def one(e, c):
            k = step * ROW + e
            to = lax.rem(g + e, ROW)
            do(pltpu.make_async_remote_copy(
                src_ref=turned.at[pl.ds(pl.multiple_of(step * row_rows + to * rows, 16), rows)],
                dst_ref=recv.at[pl.ds(pl.multiple_of(from_y(step) * row_rows + g * rows, 16), rows)],
                send_sem=s_sem.at[k], recv_sem=r_sem.at[k], device_id=at_g(e), device_id_type=MESH))
            return c
        lax.fori_loop(1, ROW, one, 0)

    def forward(parcel_now, turned, recv, s_sem, r_sem, step):
        turned[pl.ds(step * row_rows, row_rows), :] = mm(order, parcel_now).astype(BF16)
        r_each(turned, recv, s_sem, r_sem, step, begin)
        mine = pl.multiple_of(g * rows, 16)
        recv[pl.ds(pl.multiple_of(from_y(step) * row_rows, 16) + mine, rows), :] = turned[
            pl.ds(step * row_rows + mine, rows), :]

    set_a = (pack_a, leg_a, ya_send, ya_recv)
    set_d = (pack_d, leg_d, yd_send, yd_recv)
    next_a = (turn_a, recv_a, ra_send, ra_recv)
    next_d = (turn_d, recv_d, rd_send, rd_recv)
    here = pl.ds(pl.multiple_of(y * parcel, 16), parcel)

    def arrive(first, second, step):
        y_copy(*first, step).wait_recv()
        forward(first[1][pl.ds(step * parcel, parcel), :], *second, step)

    for step in z_order:
        z_copy(step).start()
    pack_a[...] = mm(pick[...], amp_ref[...]).astype(BF16)
    for step in y_order:
        y_copy(*set_a, step).start()

    spread(local[...], narrow * share)
    tiles[ki] = jnp.zeros((TILE, 128), BF16)
    want = hot(iota((row_rows, pairs * kt), 0) + y * row_rows == slot)
    order = lax.dot_general(want, pick[here, :], NT, preferred_element_type=F32).astype(BF16)

    codes = codes_ref[...]
    second = lax.rem(codes, NVT)
    odd = lax.rem(second, 2)
    cell = lax.div(second, 2) * NVT + lax.div(codes, NVT)
    match = iota((hf, kt), 0) == cell
    onto = jnp.concatenate([hot(match & (odd == 0)), hot(match & (odd == 1))], axis=1)
    lows = jnp.concatenate([low] * blocks, axis=1)
    zero = jnp.zeros((kt, cells), BF16)

    def dense_pair(p):
        a = amp_ref[pl.ds(p * kt, kt), :]
        turned = jnp.concatenate([pltpu.roll(a[:, m * 128:(m + 1) * 128], TILE, 1) for m in range(blocks)], axis=1)
        g0 = mm(onto, jnp.concatenate([jnp.where(lows, a, zero), jnp.where(lows, zero, turned)], axis=0))
        g1 = mm(onto, jnp.concatenate([jnp.where(lows, turned, zero), jnp.where(lows, zero, a)], axis=0))
        for m in range(blocks):
            for h in range(NVT // 2):
                both = jnp.concatenate([v[h * NVT:(h + 1) * NVT, m * 128:(m + 1) * 128] for v in (g0, g1)], axis=0)
                adense[pl.ds((p * blocks + m) * 2 * NVT, 2 * NVT), pl.ds(h * 128, 128)] = both.astype(BF16)

    todo = list(range(pairs))
    for i, step in enumerate(z_order):
        if i % 2 == 0 and todo:
            dense_pair(todo.pop(0))
        z_copy(step).wait_recv()
        for e in mates:
            x_copy(step, e).start()
        c_copy(step, 0).start()
    for p in todo:
        dense_pair(p)
    forward(pack_a[here, :], *next_a, 0)
    for step in z_order:
        for e in mates:
            x_copy(step, e).wait_recv()
            c_copy(step, e).start()
    for step in z_order:
        for e in (0, *mates):
            c_copy(step, e).wait_recv()
        spread(gath[pl.ds(pl.multiple_of(from_z(step) * share * 32, 16), share * 32), :], from_z(step) * share)

    def gather_row(c, carry):
        for h in range(NVT // 2):
            l = tiles[table_ref[c * NVT + 2 * h]]
            r = tiles[table_ref[c * NVT + 2 * h + 1]]
            idense[pl.ds(pl.multiple_of(c * TILE, TILE), TILE), pl.ds(h * 128, 128)] = jnp.where(low, l, r)
        return carry

    lax.fori_loop(0, NVT, gather_row, 0)

    def product(n, carry):
        rhs = idense[pl.ds(pl.multiple_of(n * 256, 256), 256), :]
        d = lax.dot_general(adense[...], rhs, NT, preferred_element_type=F32)
        for p in range(pairs):
            for a in range(2 * blocks):
                x = d[(p * 2 * blocks + a) * NVT:(p * 2 * blocks + a + 1) * NVT]
                both = jnp.concatenate([x[:, :128], x[:, 128:]], axis=0).astype(BF16)
                zbuf[p, pl.ds(pl.multiple_of(n * 2 * NVT, 16), 2 * NVT), pl.ds(a * 128, 128)] = both
        return carry

    lax.fori_loop(0, NVT // 4, product, 0)

    cell_col, odd_col = column_of(cell), column_of(odd)
    match = iota((kt, hf), 1) == cell_col
    take = jnp.concatenate([hot(match & (odd_col == 0)), hot(match & (odd_col == 1))], axis=0)
    u, v = iota((512, 128), 0), iota((512, 128), 1)
    goal = ((u >> 7) & 1) * TILE + (u & 31) * 2 + ((u >> 5) & 1)
    back = hot((v == goal) & (((u >> 8) & 1) == ((u >> 6) & 1)))
    for p in range(pairs):
        got = mm(take, zbuf[p]).astype(BF16)
        for m in range(blocks):
            part_m = got[:, m * 256:(m + 1) * 256]
            flat = jnp.concatenate([part_m[:kt], part_m[kt:]], axis=1)
            dress[pl.ds(p * kt, kt), pl.ds(m * 128, 128)] = mm(flat, back).astype(BF16)
    pack_d[...] = mm(pick[...], dress[...]).astype(BF16)
    for step in y_order:
        y_copy(*set_d, step).start()

    for step in y_order:
        arrive(set_a, next_a, step)
    forward(pack_d[here, :], *next_d, 0)

    total = wn * rows
    np_all = hole_ref.shape[0]
    r0, c0 = iota((total, np_all), 0), iota((total, np_all), 1)
    by_row = mm(hot(lax.div(r0, CAP) == c0), hole_ref[...]).astype(BF16)
    r1, c1 = iota((np_all, total), 0), iota((np_all, total), 1)
    by_col = hot(lax.div(c1, rows) * pairs + lax.rem(c1, pairs) == r1)
    r2, c2 = iota((row_rows, total), 0), iota((row_rows, total), 1)
    same = lax.rem(r2, CAP) == lax.rem(lax.div(c2, pairs), CAP)
    for i in range(yn):
        hexp[pl.ds(i * row_rows, row_rows), :] = jnp.where(
            same, mm(by_row[i * row_rows:(i + 1) * row_rows], by_col), 0.0).astype(BF16)
    for step in [0] + y_order:
        r_each(*next_a, step, landed)

    def ladder(i, carry):
        at = pl.ds(pl.multiple_of(i * row_rows, 16), row_rows)
        acc[at, :] = mm(hexp[at, :], recv_a[...])
        return carry

    lax.fori_loop(0, yn, ladder, 0)

    r3, c3 = iota((row_rows, row_rows), 0), iota((row_rows, row_rows), 1)
    source = lax.div(r3, rows) * rows + lax.rem(r3, CAP) * pairs + lax.rem(lax.div(r3, CAP), pairs)
    swap = hot(c3 == source)

    def finish(step):
        r_each(*next_d, step, landed)
        at = pl.ds(pl.multiple_of(from_y(step) * row_rows, 16), row_rows)
        done = (acc[at, :] + mm(swap, recv_d[at, :])).astype(BF16)
        out_ref[pl.ds(from_y(step) * ROW * pairs, ROW * pairs)] = done.reshape(ROW * pairs, CAP, cells)

    waiting = [0]
    for step in y_order:
        arrive(set_d, next_d, step)
        finish(waiting.pop())
        waiting.append(step)
    finish(waiting.pop())

    for step in z_order:
        z_copy(step).wait_send()
        c_copy(step, 0).wait_send()
        for e in mates:
            x_copy(step, e).wait_send()
            c_copy(step, e).wait_send()
    for step in y_order:
        y_copy(*set_a, step).wait_send()
        y_copy(*set_d, step).wait_send()
    for step in [0] + y_order:
        r_each(*next_a, step, left)
        r_each(*next_d, step, left)


def run(wn, zn, number, room, table, amps, ints, hole, codes, owner):
    cells = amps.shape[1]
    share = ints.shape[0]
    ki = share * zn
    pairs = hole.shape[0] // wn
    total = wn * CAP * pairs
    yn = wn // ROW
    blocks = cells // 128
    packed = yn * room * pairs
    vmem = pl.BlockSpec(memory_space=pltpu.VMEM)
    dma = pltpu.SemaphoreType.DMA
    return pl.pallas_call(
        functools.partial(kernel, wn, zn, room),
        out_shape=jax.ShapeDtypeStruct((wn * pairs, CAP, cells), BF16),
        in_specs=[pl.BlockSpec(memory_space=pltpu.SMEM)] + [vmem] * 5,
        out_specs=vmem,
        scratch_shapes=[
            pltpu.VMEM((share * 32, 128), BF16),
            pltpu.VMEM((share * 32, 128), F32),
            pltpu.VMEM((ki * 32, 128), BF16),
            pltpu.VMEM((ki + 1, TILE, 128), BF16),
            pltpu.VMEM((NVT * TILE, NVT * TILE), BF16),
            pltpu.VMEM((pairs * blocks * 2 * NVT, NVT * TILE), BF16),
            pltpu.VMEM((pairs, NVT * NVT // 2, 2 * cells), BF16),
            pltpu.VMEM(amps.shape, BF16),
            pltpu.VMEM((packed, amps.shape[0]), BF16),
        ] + [pltpu.VMEM((packed, cells), BF16)] * 4 + [pltpu.VMEM((total, cells), BF16)] * 4 + [
            pltpu.VMEM((total, total), BF16),
            pltpu.VMEM((total, cells), F32),
        ] + [dma((zn,))] * 2 + [dma((zn * ROW,))] * 4 + [dma((yn,))] * 4 + [dma((yn * ROW,))] * 4,
        compiler_params=pltpu.CompilerParams(
            collective_id=number, has_side_effects=True, vmem_limit_bytes=58 * 1024 * 1024
        ),
        cost_estimate=pl.CostEstimate(flops=8 * 10**9, bytes_accessed=4 * 10**6, transcendentals=0),
    )(table, amps, ints, hole, codes, owner)


def per_device(wn, zn, amplitudes, int_values, hole_ladder, amp_tiles, int_tiles, owner):
    pairs, kt, cells = amplitudes.shape
    ki = int_values.shape[0] * zn
    yn = wn // ROW
    matches = jnp.arange(NVT * NVT, dtype=I32)[:, None] == int_tiles[None, :]
    table = ki + jnp.sum(jnp.where(matches, jnp.arange(ki, dtype=I32)[None, :] - ki, 0), axis=1)
    fill = jnp.sum((owner // ROW == jnp.arange(yn, dtype=I32)[None, :]).astype(I32), axis=0)
    most = jnp.max(fill)
    rooms = tuple(r * ROW * CAP // 32 for r in ROOMS)
    branch = sum((most > r).astype(I32) for r in rooms[:-1])
    return lax.switch(
        branch,
        [functools.partial(run, wn, zn, i, room) for i, room in enumerate(rooms)],
        table,
        amplitudes.reshape(pairs * kt, cells),
        int_values,
        hole_ladder,
        amp_tiles.reshape(1, kt),
        owner.reshape(1, kt),
    )


def solution(mesh):
    wn, zn = mesh.shape["wide"], mesh.shape["narrow"]
    return jax.shard_map(
        functools.partial(per_device, wn, zn),
        mesh=mesh,
        in_specs=(P("wide", None, "narrow"), P("narrow", None), P(), P(), P(), P()),
        out_specs=P(None, "wide", "narrow"),
        check_vma=False,
    )
```

time: 227 us -> 86 us (0.38)
  local copies, waits for them, and re-layouts: 103 us -> 1.84 us
  Pallas kernels: 0 us -> 80.1 us
  waiting for transfers between devices: 76.9 us -> 0 us
  starting transfers between devices: 20.9 us -> 0 us
  between operations: 13.8 us -> 1.36 us
  matrix products: 5.73 us -> 0 us
  other arithmetic: 4.96 us -> 2.26 us
    pallas_call x0 -> x1, Pallas kernels: none -> 80.1 us  [run(): pl.pallas_call(functools.partial(kernel, wn, zn, room), out_shape=jax.Sha...]
    reshape x10 -> x0, local copies, waits for them, and re-layouts: 71.7 us -> none  [the longest x2 42.5 us: per_device(): right_tiles = int_pad[int_ids].reshape(NVT, row_most, row_most, TILE, TILE)]
    all_to_all x2 -> x0, waiting for transfers between devices: 48.3 us -> none  [the longest x1 24.9 us: per_device(): lax.all_to_all(send_dressed, 'wide', split_axis=1, concat_axis=0, tiled=T...]
    all_gather x1 -> x0, waiting for transfers between devices: 27.8 us -> none  [per_device(): int_all = lax.all_gather(int_values, 'narrow', axis=0, tiled=True)]
    gather x8 -> x0, local copies, waits for them, and re-layouts: 20.9 us -> none  [the longest x1 6.55 us: per_device(): right_tiles = int_pad[int_ids].reshape(NVT, row_most, row_most, TILE, TILE)]
    all_to_all x2 -> x0, starting transfers between devices: 20.9 us -> none  [the longest x1 14.4 us: per_device(): lax.all_to_all(send_dressed, 'wide', split_axis=1, concat_axis=0, tiled=T...]
    convert_element_type x3 -> x0, local copies, waits for them, and re-layouts: 6.87 us -> none  [the longest x2 4.24 us: per_device(): dress_part.astype(jnp.float32)]
    dot_general x2 -> x0, matrix products: 5.73 us -> none  [the longest x1 4.15 us: per_device(): jnp.einsum('rmx,rxy->rmy', left_matrix, right_matrix, preferred_element_t...]
  transfers between devices with their start and end apart: 3 -> 0, of which waited for: 3 -> 0; matrix products, arithmetic and copies ran while one was open for 12% -> 0% of each run, Pallas kernels for 0% -> 0%
where the time goes in v2:
time: 86 us; the launch traced here: 85.8 us
  Pallas kernels  80.1 us (93%)
  other arithmetic  2.26 us (3%)
  local copies, waits for them, and re-layouts  1.84 us (2%)
  between operations  1.36 us (2%)
    pallas_call x1, Pallas kernels, run(): pl.pallas_call(functools.partial(kernel, wn, zn, room), out_shape=jax.Sha...  80.1 us

profile of v2, /device:TPU:1, one launch (start us, length us, event | category | flops | bytes accessed | tf_op | source)
XLA Modules:
  0.0 85.8 jit_solution(9433597438576044335)
XLA Ops:
  0.0 0.0 copy-start.1
  0.0 0.7 fusion
  0.7 0.1 convert_reduce_fusion
  0.8 0.6 reduce_max.9
  2.8 0.0 copy-start
  2.8 0.0 copy-start.8
  2.8 0.0 copy-start.9
  2.9 0.0 copy-done.1
  2.9 0.6 copy-done
  3.5 0.0 copy-done.8
  3.5 0.0 copy-done.9
  3.5 81.3 %conditional.1 = (bf16[256,4,512]{2,1,0:T(4,128)(2,1)S(1)}) conditional(s32[]{:T(128)} %clamp.3, (s32[576,192]{1,0:T(8,128)S(1)}, bf16[4,128,512]{2,1,0:T(8,128)(2,1)S(1)}, bf16[24,4096]{1,0:T(8,128)(2,1)}, bf16[256,256]{1,0:T(8,128)(2,1)}, s32[128]{0:T(128)S(1)}, /*index=5*/s32[128,1]{0,1:T(1,128)S(1)}, s32[]{:T(128)}, ...), branch_computations={%region_3.4_spmd.clone, %region_4.5_spmd.clone, %region_5.6_spmd.c... | conditional | flops 8000331776 | bytes 5763144 | solution.py:373
  3.5 0.0 copy-start.2
  3.5 0.0 copy-start.5
  3.5 0.2 select_reduce_fusion
  3.7 0.6 broadcast_add_fusion.table_ref
  4.3 0.1 copy-done.2
  4.4 0.1 copy-done.5
  4.5 80.1 %branch_0_fun.1 = bf16[256,4,512]{2,1,0:T(4,128)(2,1)S(1)} custom-call(s32[576]{0:T(1024)} %broadcast_add_fusion.table_ref, bf16[512,512]{1,0:T(8,128)(2,1)S(1)} %bitcast.11, bf16[24,4096]{1,0:T(8,128)(2,1)S(1)} %copy-done.2, bf16[256,256]{1,0:T(8,128)(2,1)S(1)} %copy-done.5, s32[1,128]{1,0:T(1,128)S(1)} %bitcast.17, s32[1,128]{1,0:T(1,128)S(1)} %bitcast.14), custom_call_target="tpu_custom_call" | custom-call | flops 8000000000 | bytes 4000000 | tf_op jit(solution)/shard_map/cond/branch_0_fun/pallas_call | solution.py:337
  84.8 1.0 %copy.47 = bf16[256,4,512]{2,1,0:T(4,128)(2,1)} copy(bf16[256,4,512]{2,1,0:T(4,128)(2,1)S(1)} %get-tuple-element.63) | data formatting | bytes 2097152
  (3 shorter events, 0.0 us)
Async XLA Ops:
  0.0 2.9 %copy-start.1 = (bf16[4,128,512]{2,1,0:T(8,128)(2,1)S(1)}, bf16[4,128,512]{2,1,0:T(8,128)(2,1)}, u32[]{:S(2)}) copy-start(bf16[4,128,512]{2,1,0:T(8,128)(2,1)} %param.9) | copy-start | bytes 1572868
  2.8 0.7 copy-start
  2.8 0.7 copy-start.8
  2.8 0.7 copy-start.9
  3.5 0.9 %copy-start.2 = (bf16[24,4096]{1,0:T(8,128)(2,1)S(1)}, bf16[24,4096]{1,0:T(8,128)(2,1)}, u32[]{:S(2)}) copy-start(bf16[24,4096]{1,0:T(8,128)(2,1)} %get-tuple-element.153.int_ref) | copy-start | bytes 589828 | tf_op jit(solution)/shard_map/cond
  3.5 1.0 %copy-start.5 = (bf16[256,256]{1,0:T(8,128)(2,1)S(1)}, bf16[256,256]{1,0:T(8,128)(2,1)}, u32[]{:S(2)}) copy-start(bf16[256,256]{1,0:T(8,128)(2,1)} %get-tuple-element.154.hole_ref) | copy-start | bytes 393220 | tf_op jit(solution)/shard_map/cond

commit v3 on v2

--- a/solution.py
+++ b/solution.py
@@ -35,27 +35,15 @@
     return jnp.sum(jnp.where(eye, row, 0), axis=1, keepdims=True)
 
 
-def far_first(n):
-    return sorted(range(1, n), key=lambda d: (-min(d, n - d), d))
-
-
-def begin(copy):
-    copy.start()
-
-
-def landed(copy):
-    copy.wait_recv()
-
-
-def left(copy):
-    copy.wait_send()
+def near_first(n):
+    return sorted(range(1, n), key=lambda d: (min(d, n - d), d))
 
 
 def kernel(wn, zn, room, table_ref, amp_ref, int_ref, hole_ref, codes_ref, owner_ref, out_ref,
            local, local32, gath, tiles, idense, adense, zbuf, dress, pick, pack_a, pack_d, leg_a, leg_d,
-           turn_a, turn_d, recv_a, recv_d, hexp, acc,
-           z_send, z_recv, x_send, x_recv, c_send, c_recv,
-           ya_send, ya_recv, yd_send, yd_recv, ra_send, ra_recv, rd_send, rd_recv):
+           turn_a, turn_d, stage_a, stage_d, recv_a, recv_d, hexp, acc,
+           z_send, z_recv, x_send, x_recv, c_send, c_recv, ya_send, ya_recv, yd_send, yd_recv,
+           ra_send, ra_recv, rd_send, rd_recv, ca_send, ca_recv, cd_send, cd_recv):
     wide = lax.axis_index("wide")
     narrow = lax.axis_index("narrow")
     yn = wn // ROW
@@ -75,7 +63,7 @@
     cells_all = NVT * NVT
     hf = cells_all // 2
     low = iota((1, 128), 1) < TILE
-    y_order, z_order = far_first(yn), far_first(zn)
+    y_order, z_order = near_first(yn), near_first(zn)
     mates = range(2, ROW, 2)
 
     def at_y(step):
@@ -152,33 +140,54 @@
     def from_y(step):
         return lax.rem(y + yn - step, yn)
 
-    def r_each(turned, recv, s_sem, r_sem, step, do):
-        def one(e, c):
-            k = step * ROW + e
-            to = lax.rem(g + e, ROW)
-            do(pltpu.make_async_remote_copy(
-                src_ref=turned.at[pl.ds(pl.multiple_of(step * row_rows + to * rows, 16), rows)],
-                dst_ref=recv.at[pl.ds(pl.multiple_of(from_y(step) * row_rows + g * rows, 16), rows)],
-                send_sem=s_sem.at[k], recv_sem=r_sem.at[k], device_id=at_g(e), device_id_type=MESH))
-            return c
-        lax.fori_loop(1, ROW, one, 0)
-
-    def forward(parcel_now, turned, recv, s_sem, r_sem, step):
+    def r_copy(turned, stage, recv, r_s, r_r, c_s, c_r, step, e):
+        k = step * ROW + e
+        to = lax.div(lax.rem(g + e, ROW), 2)
+        return pltpu.make_async_remote_copy(
+            src_ref=turned.at[pl.ds(pl.multiple_of(step * row_rows + to * 2 * rows, 16), 2 * rows)],
+            dst_ref=stage.at[pl.ds(k * rows, 2 * rows)],
+            send_sem=r_s.at[k], recv_sem=r_r.at[k], device_id=at_g(e), device_id_type=MESH)
+
+    def h_copy(turned, stage, recv, r_s, r_r, c_s, c_r, step, e):
+        k = step * ROW + e
+        if e == 0:
+            src = turned.at[pl.ds(pl.multiple_of(step * row_rows + lax.rem(other, ROW) * rows, 16), rows)]
+        else:
+            src = stage.at[pl.ds(pl.multiple_of(k * rows + lax.rem(other, 2) * rows, 16), rows)]
+        return pltpu.make_async_remote_copy(
+            src_ref=src, dst_ref=recv.at[recv_at(step, e)],
+            send_sem=c_s.at[k], recv_sem=c_r.at[k], device_id=(other, narrow), device_id_type=MESH)
+
+    def recv_at(step, e):
+        return pl.ds(pl.multiple_of(from_y(step) * row_rows + lax.rem(g + ROW - e, ROW) * rows, 16), rows)
+
+    def forward(parcel_now, step, turned, stage, recv, *sems):
         turned[pl.ds(step * row_rows, row_rows), :] = mm(order, parcel_now).astype(BF16)
-        r_each(turned, recv, s_sem, r_sem, step, begin)
-        mine = pl.multiple_of(g * rows, 16)
-        recv[pl.ds(pl.multiple_of(from_y(step) * row_rows, 16) + mine, rows), :] = turned[
-            pl.ds(step * row_rows + mine, rows), :]
+        for e in mates:
+            r_copy(turned, stage, recv, *sems, step, e).start()
+        h_copy(turned, stage, recv, *sems, step, 0).start()
+        recv[recv_at(step, 0), :] = turned[pl.ds(pl.multiple_of(step * row_rows + g * rows, 16), rows), :]
+
+    def relay(step, turned, stage, recv, *sems):
+        for e in mates:
+            r_copy(turned, stage, recv, *sems, step, e).wait_recv()
+            h_copy(turned, stage, recv, *sems, step, e).start()
+            at = pl.multiple_of((step * ROW + e) * rows + lax.rem(g, 2) * rows, 16)
+            recv[recv_at(step, e), :] = stage[pl.ds(at, rows), :]
+
+    def settle(step, *second):
+        for e in (0, *mates):
+            h_copy(*second, step, e).wait_recv()
 
     set_a = (pack_a, leg_a, ya_send, ya_recv)
     set_d = (pack_d, leg_d, yd_send, yd_recv)
-    next_a = (turn_a, recv_a, ra_send, ra_recv)
-    next_d = (turn_d, recv_d, rd_send, rd_recv)
+    next_a = (turn_a, stage_a, recv_a, ra_send, ra_recv, ca_send, ca_recv)
+    next_d = (turn_d, stage_d, recv_d, rd_send, rd_recv, cd_send, cd_recv)
     here = pl.ds(pl.multiple_of(y * parcel, 16), parcel)
 
-    def arrive(first, second, step):
+    def arrive(step, first, second):
         y_copy(*first, step).wait_recv()
-        forward(first[1][pl.ds(step * parcel, parcel), :], *second, step)
+        forward(first[1][pl.ds(step * parcel, parcel), :], step, *second)
 
     for step in z_order:
         z_copy(step).start()
@@ -218,22 +227,35 @@
         for e in mates:
             x_copy(step, e).start()
         c_copy(step, 0).start()
+        if i >= 2:
+            for e in mates:
+                x_copy(z_order[i - 2], e).wait_recv()
+                c_copy(z_order[i - 2], e).start()
     for p in todo:
         dense_pair(p)
-    forward(pack_a[here, :], *next_a, 0)
-    for step in z_order:
+    for step in z_order[-2:]:
         for e in mates:
             x_copy(step, e).wait_recv()
             c_copy(step, e).start()
+    forward(pack_a[here, :], 0, *next_a)
+    early = (len(y_order) + 1) // 2
+    coming, going = y_order[:early], [0]
     for step in z_order:
+        if coming:
+            arrive(coming[0], set_a, next_a)
+            going.append(coming.pop(0))
         for e in (0, *mates):
             c_copy(step, e).wait_recv()
         spread(gath[pl.ds(pl.multiple_of(from_z(step) * share * 32, 16), share * 32), :], from_z(step) * share)
+    for step in coming:
+        arrive(step, set_a, next_a)
+        going.append(step)
+    coming = y_order[early:]
 
     def gather_row(c, carry):
         for h in range(NVT // 2):
-            l = tiles[table_ref[c * NVT + 2 * h]]
-            r = tiles[table_ref[c * NVT + 2 * h + 1]]
+            l = tiles[table_ref[0, c * NVT + 2 * h]]
+            r = tiles[table_ref[0, c * NVT + 2 * h + 1]]
             idense[pl.ds(pl.multiple_of(c * TILE, TILE), TILE), pl.ds(h * 128, 128)] = jnp.where(low, l, r)
         return carry
 
@@ -249,7 +271,12 @@
                 zbuf[p, pl.ds(pl.multiple_of(n * 2 * NVT, 16), 2 * NVT), pl.ds(a * 128, 128)] = both
         return carry
 
-    lax.fori_loop(0, NVT // 4, product, 0)
+    lax.fori_loop(0, NVT // 8, product, 0)
+    for step in going:
+        relay(step, *next_a)
+    lax.fori_loop(NVT // 8, NVT // 4, product, 0)
+    for step in coming:
+        arrive(step, set_a, next_a)
 
     cell_col, odd_col = column_of(cell), column_of(odd)
     match = iota((kt, hf), 1) == cell_col
@@ -267,9 +294,9 @@
     for step in y_order:
         y_copy(*set_d, step).start()
 
-    for step in y_order:
-        arrive(set_a, next_a, step)
-    forward(pack_d[here, :], *next_d, 0)
+    for step in coming:
+        relay(step, *next_a)
+    forward(pack_d[here, :], 0, *next_d)
 
     total = wn * rows
     np_all = hole_ref.shape[0]
@@ -283,7 +310,7 @@
         hexp[pl.ds(i * row_rows, row_rows), :] = jnp.where(
             same, mm(by_row[i * row_rows:(i + 1) * row_rows], by_col), 0.0).astype(BF16)
     for step in [0] + y_order:
-        r_each(*next_a, step, landed)
+        settle(step, *next_a)
 
     def ladder(i, carry):
         at = pl.ds(pl.multiple_of(i * row_rows, 16), row_rows)
@@ -297,17 +324,21 @@
     swap = hot(c3 == source)
 
     def finish(step):
-        r_each(*next_d, step, landed)
+        settle(step, *next_d)
         at = pl.ds(pl.multiple_of(from_y(step) * row_rows, 16), row_rows)
         done = (acc[at, :] + mm(swap, recv_d[at, :])).astype(BF16)
         out_ref[pl.ds(from_y(step) * ROW * pairs, ROW * pairs)] = done.reshape(ROW * pairs, CAP, cells)
 
-    waiting = [0]
-    for step in y_order:
-        arrive(set_d, next_d, step)
-        finish(waiting.pop())
-        waiting.append(step)
-    finish(waiting.pop())
+    line_up = [0] + y_order
+    for i, step in enumerate(line_up):
+        if i >= 1:
+            arrive(step, set_d, next_d)
+            relay(line_up[i - 1], *next_d)
+        if i >= 2:
+            finish(line_up[i - 2])
+    relay(line_up[-1], *next_d)
+    for step in line_up[-2:]:
+        finish(step)
 
     for step in z_order:
         z_copy(step).wait_send()
@@ -319,8 +350,22 @@
         y_copy(*set_a, step).wait_send()
         y_copy(*set_d, step).wait_send()
     for step in [0] + y_order:
-        r_each(*next_a, step, left)
-        r_each(*next_d, step, left)
+        for second in (next_a, next_d):
+            h_copy(*second, step, 0).wait_send()
+            for e in mates:
+                r_copy(*second, step, e).wait_send()
+                h_copy(*second, step, e).wait_send()
+
+
+def prepare(wn, rooms, codes_ref, owner_ref, table_ref, branch_ref):
+    ki, kt = codes_ref.shape[1], owner_ref.shape[1]
+    codes = column_of(codes_ref[...])
+    found = codes == iota((ki, NVT * NVT), 1)
+    table_ref[...] = ki + jnp.sum(jnp.where(found, iota((ki, NVT * NVT), 0) - ki, 0), axis=0, keepdims=True)
+    line = lax.div(owner_ref[...], ROW)
+    fill = jnp.sum(jnp.where(line == iota((wn // ROW, kt), 0), 1, 0), axis=1, keepdims=True)
+    most = jnp.max(fill, axis=0, keepdims=True)
+    branch_ref[...] = sum(jnp.where(most > r, 1, 0) for r in rooms[:-1])
 
 
 def run(wn, zn, number, room, table, amps, ints, hole, codes, owner):
@@ -349,10 +394,10 @@
             pltpu.VMEM((pairs, NVT * NVT // 2, 2 * cells), BF16),
             pltpu.VMEM(amps.shape, BF16),
             pltpu.VMEM((packed, amps.shape[0]), BF16),
-        ] + [pltpu.VMEM((packed, cells), BF16)] * 4 + [pltpu.VMEM((total, cells), BF16)] * 4 + [
+        ] + [pltpu.VMEM((packed, cells), BF16)] * 4 + [pltpu.VMEM((total, cells), BF16)] * 6 + [
             pltpu.VMEM((total, total), BF16),
             pltpu.VMEM((total, cells), F32),
-        ] + [dma((zn,))] * 2 + [dma((zn * ROW,))] * 4 + [dma((yn,))] * 4 + [dma((yn * ROW,))] * 4,
+        ] + [dma((zn,))] * 2 + [dma((zn * ROW,))] * 4 + [dma((yn,))] * 4 + [dma((yn * ROW,))] * 8,
         compiler_params=pltpu.CompilerParams(
             collective_id=number, has_side_effects=True, vmem_limit_bytes=58 * 1024 * 1024
         ),
@@ -363,22 +408,23 @@
 def per_device(wn, zn, amplitudes, int_values, hole_ladder, amp_tiles, int_tiles, owner):
     pairs, kt, cells = amplitudes.shape
     ki = int_values.shape[0] * zn
-    yn = wn // ROW
-    matches = jnp.arange(NVT * NVT, dtype=I32)[:, None] == int_tiles[None, :]
-    table = ki + jnp.sum(jnp.where(matches, jnp.arange(ki, dtype=I32)[None, :] - ki, 0), axis=1)
-    fill = jnp.sum((owner // ROW == jnp.arange(yn, dtype=I32)[None, :]).astype(I32), axis=0)
-    most = jnp.max(fill)
     rooms = tuple(r * ROW * CAP // 32 for r in ROOMS)
-    branch = sum((most > r).astype(I32) for r in rooms[:-1])
+    codes, owner = int_tiles.reshape(1, ki), owner.reshape(1, kt)
+    table, branch = pl.pallas_call(
+        functools.partial(prepare, wn, rooms),
+        out_shape=(jax.ShapeDtypeStruct((1, NVT * NVT), I32), jax.ShapeDtypeStruct((1, 1), I32)),
+        in_specs=[pl.BlockSpec(memory_space=pltpu.VMEM)] * 2,
+        out_specs=(pl.BlockSpec(memory_space=pltpu.VMEM), pl.BlockSpec(memory_space=pltpu.VMEM)),
+    )(codes, owner)
     return lax.switch(
-        branch,
+        branch[0, 0],
         [functools.partial(run, wn, zn, i, room) for i, room in enumerate(rooms)],
         table,
         amplitudes.reshape(pairs * kt, cells),
         int_values,
         hole_ladder,
         amp_tiles.reshape(1, kt),
-        owner.reshape(1, kt),
+        owner,
     )
 
 

time: 86 us -> 85.1 us (0.990)
  other arithmetic: 2.26 us -> 0 us
  Pallas kernels: 80.1 us -> 81.8 us
    pallas_call x0 -> x1, Pallas kernels: none -> 1.35 us  [per_device(): pl.pallas_call(functools.partial(prepare, wn, rooms), out_shape=(jax.Shap...]
    unnamed x9 -> x5, local copies, waits for them, and re-layouts: 1.58 us -> 2.28 us
where the time goes in v3:
time: 85.1 us; the launch traced here: 85 us
  Pallas kernels  81.8 us (96%)
  local copies, waits for them, and re-layouts  2.28 us (3%)
    pallas_call x1, Pallas kernels, run(): pl.pallas_call(functools.partial(kernel, wn, zn, room), out_shape=jax.Sha...  80.4 us
    unnamed x5, local copies, waits for them, and re-layouts  2.28 us

profile of v3, /device:TPU:1, one launch (start us, length us, event | category | flops | bytes accessed | tf_op | source)
XLA Modules:
  0.0 85.0 jit_solution(13233818486751645211)
XLA Ops:
  0.0 0.0 copy-start
  0.0 0.7 copy-done
  0.7 1.4 %shard_map.67 = (s32[1,576]{1,0:T(1,128)S(1)}, s32[1,1]{1,0:T(1,128)}) custom-call(s32[1,192]{1,0:T(1,128)} %bitcast.8, s32[1,128]{1,0:T(1,128)S(1)} %bitcast.9), custom_call_target="tpu_custom_call" | custom-call | tf_op jit(solution)/shard_map/pallas_call | solution.py:413
  2.7 0.0 copy-start.1
  2.7 0.6 copy-done.1
  3.3 80.7 %conditional.1 = (bf16[256,4,512]{2,1,0:T(4,128)(2,1)S(1)}) conditional(s32[]{:T(128)} %bitcast.2, (s32[1,576]{1,0:T(1,128)S(1)}, bf16[512,512]{1,0:T(8,128)(2,1)}, bf16[24,4096]{1,0:T(8,128)(2,1)}, bf16[256,256]{1,0:T(8,128)(2,1)}, s32[1,128]{1,0:T(1,128)S(1)}, /*index=5*/s32[1,128]{1,0:T(1,128)S(1)}) %tuple.27, ...), branch_computations={%region_0.0_spmd, %region_1.0_spmd, %region_2.0_spmd} | conditional | flops 8000000000 | bytes 4000008 | solution.py:419
  3.3 80.4 %branch_0_fun.1 = bf16[256,4,512]{2,1,0:T(4,128)(2,1)S(1)} custom-call(s32[1,576]{1,0:T(1,128)S(1)} %get-tuple-element.44.table_ref, bf16[512,512]{1,0:T(8,128)(2,1)} %get-tuple-element.46.amp_ref, bf16[24,4096]{1,0:T(8,128)(2,1)} %get-tuple-element.47.int_ref, bf16[256,256]{1,0:T(8,128)(2,1)} %get-tuple-element.48.hole_ref, ...), custom_call_target="tpu_custom_call" | custom-call | flops 8000000000 | bytes 4000000 | tf_op jit(solution)/shard_map/cond/branch_0_fun/pallas_call | solution.py:382
  84.0 1.0 %copy.14 = bf16[256,4,512]{2,1,0:T(4,128)(2,1)} copy(bf16[256,4,512]{2,1,0:T(4,128)(2,1)S(1)} %get-tuple-element.67) | data formatting | bytes 2097152
Async XLA Ops:
  0.0 0.7 copy-start
  2.7 0.7 copy-start.1

commit v4 on v2

v4 whole, which is shorter than its diff:
```python
import functools

import jax
import jax.numpy as jnp
from jax import lax
from jax.experimental import pallas as pl
from jax.experimental.pallas import tpu as pltpu
from jax.sharding import PartitionSpec as P

TILE = 64
NVT = 24
CAP = 4
MESH = pl.DeviceIdType.MESH
NT = (((1,), (1,)), ((), ()))
BF16, F32, I32 = jnp.bfloat16, jnp.float32, jnp.int32


def iota(shape, dim):
    return lax.broadcasted_iota(I32, shape, dim)


def hot(mask):
    return jnp.where(mask, 1.0, 0.0).astype(BF16)


def mm(a, b):
    return jnp.dot(a, b, preferred_element_type=F32)


def column_of(row):
    n = row.shape[1]
    eye = iota((n, n), 0) == iota((n, n), 1)
    return jnp.sum(jnp.where(eye, row, 0), axis=1, keepdims=True)


def near_first(n):
    return sorted(range(1, n), key=lambda d: (min(d, n - d), d))


def kernel(wn, zn, listed_ref, amp_ref, int_ref, hole_ref, codes_ref, owner_ref, out_ref,
           local, local32, gath, tiles, idense, adense, zbuf, dress, pick, send_a, send_d, recv_a, recv_d, hexp, acc,
           table_vec, table_ref, table_sem, z_send, z_recv, c_send, c_recv, a_send, a_recv, d_send, d_recv):
    wide = lax.axis_index("wide")
    narrow = lax.axis_index("narrow")
    core = lax.rem(wide, 2)
    other = wide + 1 - 2 * core
    cells = amp_ref.shape[1]
    blocks = cells // 128
    pairs = hole_ref.shape[0] // wn
    kt = amp_ref.shape[0] // pairs
    rows = CAP * pairs
    total = wn * rows
    part_rows = 8 * rows if wn % 8 == 0 else total
    ki = tiles.shape[0] - 1
    share = ki // zn
    half_rows = share * 16
    cells_all = NVT * NVT
    hf = cells_all // 2
    low = iota((1, 128), 1) < TILE
    z_order = near_first(zn)
    relays = {d: (2 if d == 3 else zn - 2) for d in z_order if min(d, zn - d) == 3}

    def at_z(step):
        return (wide, lax.rem(narrow + step, zn))

    barrier = pltpu.get_barrier_semaphore()
    peers = [d for d in z_order if d not in relays]
    for step in peers:
        pl.semaphore_signal(barrier, inc=1, device_id=at_z(step), device_id_type=MESH)

    def greet(i, c):
        pl.semaphore_signal(barrier, inc=1, device_id=(lax.rem(wide + i, wn), narrow), device_id_type=MESH)
        return c

    lax.fori_loop(1, wn, greet, 0)

    own = int_ref[...].astype(F32)
    for m in range(32):
        local32[pl.ds(m, share, stride=32), :] = own[:, m * 128:(m + 1) * 128]
    local[...] = local32[...].astype(BF16)

    owner_row = owner_ref[...]
    owner_col = column_of(owner_row)
    before = iota((kt, kt), 0) < iota((kt, kt), 1)
    count = jnp.sum(jnp.where(before & (owner_col == owner_row), 1, 0), axis=0, keepdims=True)
    slot = (owner_row * CAP + count) * pairs
    slot = jnp.concatenate([slot + p for p in range(pairs)], axis=1)
    pick[...] = hot(iota((total, pairs * kt), 0) == slot)

    pl.semaphore_wait(barrier, len(peers) + wn - 1)

    def half(shard, who):
        return pl.ds(pl.multiple_of(shard * share * 32 + who * half_rows, 16), half_rows)

    def from_z(step):
        return lax.rem(narrow + zn - step, zn)

    def z_copy(step):
        if step in relays:
            src, to = gath.at[half(from_z(relays[step]), core)], at_z(step - relays[step] + zn)
            dst = gath.at[half(from_z(relays[step]), core)]
        else:
            src, to = local.at[pl.ds(pl.multiple_of(core * half_rows, 16), half_rows)], at_z(step)
            dst = gath.at[half(narrow, core)]
        return pltpu.make_async_remote_copy(
            src_ref=src, dst_ref=dst, send_sem=z_send.at[step], recv_sem=z_recv.at[step], device_id=to,
            device_id_type=MESH)

    def c_copy(step):
        at = gath.at[half(from_z(step), core)]
        return pltpu.make_async_remote_copy(
            src_ref=at, dst_ref=at, send_sem=c_send.at[step], recv_sem=c_recv.at[step], device_id=(other, narrow),
            device_id_type=MESH)

    def spread(block, first):
        n = block.shape[0] // 32
        turned = pltpu.roll(block, TILE, 1)
        tiles[pl.ds(first, n), pl.ds(0, 32)] = jnp.where(low, block, turned).reshape(n, 32, 128)
        tiles[pl.ds(first, n), pl.ds(32, 32)] = jnp.where(low, turned, block).reshape(n, 32, 128)

    def spread_half(step, who):
        spread(gath[half(from_z(step), who), :], from_z(step) * share + who * (share // 2))

    def post(send, recv, s_sem, r_sem, do):
        def one(i, c):
            i = lax.rem(i + 3 * wn // 8, wn - 1) + 1
            to = lax.rem(wide + i, wn)
            do(pltpu.make_async_remote_copy(
                src_ref=send.at[pl.ds(pl.multiple_of(to * rows, 16), rows)],
                dst_ref=recv.at[pl.ds(pl.multiple_of(wide * rows, 16), rows)],
                send_sem=s_sem.at[i], recv_sem=r_sem.at[i], device_id=(to, narrow), device_id_type=MESH))
            return c
        lax.fori_loop(0, wn - 1, one, 0)

    set_a = (send_a, recv_a, a_send, a_recv)
    set_d = (send_d, recv_d, d_send, d_recv)
    mine = pl.ds(pl.multiple_of(wide * rows, 16), rows)

    twos = [d for d in peers if d in relays.values()]
    for step in twos:
        z_copy(step).start()
    send_a[...] = mm(pick[...], amp_ref[...]).astype(BF16)
    post(*set_a, lambda copy: copy.start())
    for step in peers:
        if step not in twos:
            z_copy(step).start()
    recv_a[mine] = send_a[mine]

    spread(local[...], narrow * share)
    tiles[ki] = jnp.zeros((TILE, 128), BF16)

    codes = codes_ref[...]
    second = lax.rem(codes, NVT)
    odd = lax.rem(second, 2)
    cell = lax.div(second, 2) * NVT + lax.div(codes, NVT)
    match = iota((hf, kt), 0) == cell
    onto = jnp.concatenate([hot(match & (odd == 0)), hot(match & (odd == 1))], axis=1)
    lows = jnp.concatenate([low] * blocks, axis=1)
    zero = jnp.zeros((kt, cells), BF16)

    def dense_pair(p):
        a = amp_ref[pl.ds(p * kt, kt), :]
        turned = jnp.concatenate([pltpu.roll(a[:, m * 128:(m + 1) * 128], TILE, 1) for m in range(blocks)], axis=1)
        g0 = mm(onto, jnp.concatenate([jnp.where(lows, a, zero), jnp.where(lows, zero, turned)], axis=0))
        g1 = mm(onto, jnp.concatenate([jnp.where(lows, turned, zero), jnp.where(lows, zero, a)], axis=0))
        for m in range(blocks):
            for h in range(NVT // 2):
                both = jnp.concatenate([v[h * NVT:(h + 1) * NVT, m * 128:(m + 1) * 128] for v in (g0, g1)], axis=0)
                adense[pl.ds((p * blocks + m) * 2 * NVT, 2 * NVT), pl.ds(h * 128, 128)] = both.astype(BF16)

    found = column_of(listed_ref[...]) == iota((ki, cells_all), 1)
    last = jnp.max(jnp.where(found, iota((ki, cells_all), 0), -1), axis=0, keepdims=True)
    table_vec[...] = jnp.where(last < 0, ki, last)
    to_scalar = pltpu.make_async_copy(table_vec, table_ref, table_sem)
    to_scalar.start()
    for p in range(pairs):
        dense_pair(p)
    to_scalar.wait()
    for step in twos:
        z_copy(step).wait_recv()
        for d in relays:
            if relays[d] == step:
                z_copy(d).start()
        c_copy(step).start()
    for step in z_order:
        if step not in twos:
            z_copy(step).wait_recv()
            c_copy(step).start()
            spread_half(step, core)
    for step in twos:
        spread_half(step, core)
    for step in z_order:
        c_copy(step).wait_recv()
        spread_half(step, 1 - core)

    def gather_rows(n):
        for c in range(4):
            for h in range(NVT // 2):
                l = tiles[table_ref[0, (n * 4 + c) * NVT + 2 * h]]
                r = tiles[table_ref[0, (n * 4 + c) * NVT + 2 * h + 1]]
                idense[pl.ds(pl.multiple_of(n * 256 + c * TILE, TILE), TILE), pl.ds(h * 128, 128)] = jnp.where(
                    low, l, r)

    gather_rows(0)

    def product(n, carry):
        rhs = idense[pl.ds(pl.multiple_of(n * 256, 256), 256), :]
        d = lax.dot_general(adense[...], rhs, NT, preferred_element_type=F32)
        gather_rows(lax.rem(n + 1, NVT // 4))
        for p in range(pairs):
            for a in range(2 * blocks):
                x = d[(p * 2 * blocks + a) * NVT:(p * 2 * blocks + a + 1) * NVT]
                both = jnp.concatenate([x[:, :128], x[:, 128:]], axis=0).astype(BF16)
                zbuf[p, pl.ds(pl.multiple_of(n * 2 * NVT, 16), 2 * NVT), pl.ds(a * 128, 128)] = both
        return carry

    lax.fori_loop(0, NVT // 4, product, 0)

    cell_col, odd_col = column_of(cell), column_of(odd)
    match = iota((kt, hf), 1) == cell_col
    take = jnp.concatenate([hot(match & (odd_col == 0)), hot(match & (odd_col == 1))], axis=0)
    u, v = iota((512, 128), 0), iota((512, 128), 1)
    goal = ((u >> 7) & 1) * TILE + (u & 31) * 2 + ((u >> 5) & 1)
    back = hot((v == goal) & (((u >> 8) & 1) == ((u >> 6) & 1)))
    for p in range(pairs):
        got = mm(take, zbuf[p]).astype(BF16)
        for m in range(blocks):
            part_m = got[:, m * 256:(m + 1) * 256]
            flat = jnp.concatenate([part_m[:kt], part_m[kt:]], axis=1)
            dress[pl.ds(p * kt, kt), pl.ds(m * 128, 128)] = mm(flat, back).astype(BF16)
    send_d[...] = mm(pick[...], dress[...]).astype(BF16)
    post(*set_d, lambda copy: copy.start())
    recv_d[mine] = send_d[mine]

    np_all = hole_ref.shape[0]
    r0, c0 = iota((total, np_all), 0), iota((total, np_all), 1)
    by_row = mm(hot(lax.div(r0, CAP) == c0), hole_ref[...]).astype(BF16)
    r1, c1 = iota((np_all, total), 0), iota((np_all, total), 1)
    by_col = hot(lax.div(c1, rows) * pairs + lax.rem(c1, pairs) == r1)
    r2, c2 = iota((part_rows, total), 0), iota((part_rows, total), 1)
    same = lax.rem(r2, CAP) == lax.rem(lax.div(c2, pairs), CAP)
    for i in range(total // part_rows):
        hexp[pl.ds(i * part_rows, part_rows), :] = jnp.where(
            same, mm(by_row[i * part_rows:(i + 1) * part_rows], by_col), 0.0).astype(BF16)
    post(*set_a, lambda copy: copy.wait_recv())

    def ladder(i, carry):
        at = pl.ds(pl.multiple_of(i * part_rows, 16), part_rows)
        acc[at, :] = mm(hexp[at, :], recv_a[...])
        return carry

    lax.fori_loop(0, total // part_rows, ladder, 0)

    r3, c3 = iota((part_rows, part_rows), 0), iota((part_rows, part_rows), 1)
    source = lax.div(r3, rows) * rows + lax.rem(r3, CAP) * pairs + lax.rem(lax.div(r3, CAP), pairs)
    swap = hot(c3 == source)

    post(*set_d, lambda copy: copy.wait_recv())

    def finish(i, carry):
        at = pl.ds(pl.multiple_of(i * part_rows, 16), part_rows)
        done = (acc[at, :] + mm(swap, recv_d[at, :])).astype(BF16)
        out_ref[pl.ds(i * (part_rows // CAP), part_rows // CAP)] = done.reshape(part_rows // CAP, CAP, cells)
        return carry

    lax.fori_loop(0, total // part_rows, finish, 0)

    for step in z_order:
        z_copy(step).wait_send()
        c_copy(step).wait_send()
    post(*set_a, lambda copy: copy.wait_send())
    post(*set_d, lambda copy: copy.wait_send())


def run(wn, zn, listed, amps, ints, hole, codes, owner):
    cells = amps.shape[1]
    share = ints.shape[0]
    ki = share * zn
    pairs = hole.shape[0] // wn
    total = wn * CAP * pairs
    blocks = cells // 128
    vmem = pl.BlockSpec(memory_space=pltpu.VMEM)
    dma = pltpu.SemaphoreType.DMA
    return pl.pallas_call(
        functools.partial(kernel, wn, zn),
        out_shape=jax.ShapeDtypeStruct((wn * pairs, CAP, cells), BF16),
        in_specs=[vmem] * 6,
        out_specs=vmem,
        scratch_shapes=[
            pltpu.VMEM((share * 32, 128), BF16),
            pltpu.VMEM((share * 32, 128), F32),
            pltpu.VMEM((ki * 32, 128), BF16),
            pltpu.VMEM((ki + 1, TILE, 128), BF16),
            pltpu.VMEM((NVT * TILE, NVT * TILE), BF16),
            pltpu.VMEM((pairs * blocks * 2 * NVT, NVT * TILE), BF16),
            pltpu.VMEM((pairs, NVT * NVT // 2, 2 * cells), BF16),
            pltpu.VMEM(amps.shape, BF16),
            pltpu.VMEM((total, amps.shape[0]), BF16),
        ] + [pltpu.VMEM((total, cells), BF16)] * 4 + [
            pltpu.VMEM((total, total), BF16),
            pltpu.VMEM((total, cells), F32),
            pltpu.VMEM((1, NVT * NVT), I32),
            pltpu.SMEM((1, NVT * NVT), I32),
            dma,
        ] + [dma((zn,))] * 4 + [dma((wn,))] * 4,
        compiler_params=pltpu.CompilerParams(
            collective_id=0, has_side_effects=True, vmem_limit_bytes=58 * 1024 * 1024
        ),
        cost_estimate=pl.CostEstimate(flops=8 * 10**9, bytes_accessed=4 * 10**6, transcendentals=0),
    )(listed, amps, ints, hole, codes, owner)


def per_device(wn, zn, amplitudes, int_values, hole_ladder, amp_tiles, int_tiles, owner):
    pairs, kt, cells = amplitudes.shape
    ki = int_values.shape[0] * zn
    return run(
        wn,
        zn,
        int_tiles.reshape(1, ki),
        amplitudes.reshape(pairs * kt, cells),
        int_values,
        hole_ladder,
        amp_tiles.reshape(1, kt),
        owner.reshape(1, kt),
    )


def solution(mesh):
    wn, zn = mesh.shape["wide"], mesh.shape["narrow"]
    return jax.shard_map(
        functools.partial(per_device, wn, zn),
        mesh=mesh,
        in_specs=(P("wide", None, "narrow"), P("narrow", None), P(), P(), P(), P()),
        out_specs=P(None, "wide", "narrow"),
        check_vma=False,
    )
```

time: 86 us -> 78.6 us (0.914)
  Pallas kernels: 80.1 us -> 75.3 us
  other arithmetic: 2.26 us -> 0 us
  between operations: 1.36 us -> 0.01 us
    pallas_call x1, Pallas kernels: 80.1 us -> 75.3 us  [run(): pl.pallas_call(functools.partial(kernel, wn, zn), out_shape=jax.ShapeDtyp...]
    unnamed x9 -> x1, local copies, waits for them, and re-layouts: 1.58 us -> 2.56 us
where the time goes in v4:
time: 78.6 us; the launch traced here: 77.8 us
  Pallas kernels  75.3 us (96%)
  local copies, waits for them, and re-layouts  2.56 us (3%)
    pallas_call x1, Pallas kernels, run(): pl.pallas_call(functools.partial(kernel, wn, zn), out_shape=jax.ShapeDtyp...  75.3 us
    unnamed x1, local copies, waits for them, and re-layouts  2.56 us

profile of v4, /device:TPU:1, one launch (start us, length us, event | category | flops | bytes accessed | tf_op | source)
XLA Modules:
  0.0 77.8 jit_solution(9592607383401478394)
XLA Ops:
  0.0 75.3 %shard_map.64 = bf16[256,4,512]{2,1,0:T(4,128)(2,1)} custom-call(s32[1,192]{1,0:T(1,128)} %bitcast.5, bf16[512,512]{1,0:T(8,128)(2,1)} %bitcast.4, bf16[24,4096]{1,0:T(8,128)(2,1)} %int_ref.1, bf16[256,256]{1,0:T(8,128)(2,1)} %hole_ref.1, s32[1,128]{1,0:T(1,128)} %bitcast.6, s32[1,128]{1,0:T(1,128)} %bitcast.7), custom_call_target="tpu_custom_call" | custom-call | flops 8000000000 | bytes 4000000 | tf_op jit(solution)/shard_map/pallas_call | solution.py:284
  75.3 2.6 %copy.8 = bf16[256,4,512]{2,1,0:T(4,128)(2,1)} copy(bf16[256,4,512]{2,1,0:T(4,128)(2,1)} %shard_map.64) | data formatting | bytes 2097152

commit v5 on v4

--- a/solution.py
+++ b/solution.py
@@ -304,7 +304,7 @@
             dma,
         ] + [dma((zn,))] * 4 + [dma((wn,))] * 4,
         compiler_params=pltpu.CompilerParams(
-            collective_id=0, has_side_effects=True, vmem_limit_bytes=58 * 1024 * 1024
+            collective_id=0, has_side_effects=True, vmem_limit_bytes=40 * 1024 * 1024
         ),
         cost_estimate=pl.CostEstimate(flops=8 * 10**9, bytes_accessed=4 * 10**6, transcendentals=0),
     )(listed, amps, ints, hole, codes, owner)

time: 78.6 us -> 78.6 us (level)
  Pallas kernels: 75.3 us -> 73.3 us
  local copies, waits for them, and re-layouts: 2.56 us -> 4.54 us
    pallas_call x1, Pallas kernels: 75.3 us -> 73.3 us  [run(): pl.pallas_call(functools.partial(kernel, wn, zn), out_shape=jax.ShapeDtyp...]
    unnamed x1 -> x13, local copies, waits for them, and re-layouts: 2.56 us -> 4.54 us
where the time goes in v5:
time: 78.6 us; the launch traced here: 77.8 us
  Pallas kernels  73.3 us (93%)
  local copies, waits for them, and re-layouts  4.54 us (6%)
    pallas_call x1, Pallas kernels, run(): pl.pallas_call(functools.partial(kernel, wn, zn), out_shape=jax.ShapeDtyp...  73.3 us
    unnamed x13, local copies, waits for them, and re-layouts  4.54 us

profile of v5, /device:TPU:1, one launch (start us, length us, event | category | flops | bytes accessed | tf_op | source)
XLA Modules:
  0.0 77.8 jit_solution(13858760272088314003)
XLA Ops:
  0.0 0.0 copy-start.5
  0.0 0.0 copy-start.3
  0.0 0.0 copy-start.4
  0.0 0.6 copy-done.5
  0.7 0.0 copy-done.3
  0.7 0.0 copy-done.4
  0.7 0.0 copy-start
  0.7 1.0 %copy-done = bf16[4,128,512]{2,1,0:T(8,128)(2,1)S(1)} copy-done((bf16[4,128,512]{2,1,0:T(8,128)(2,1)S(1)}, bf16[4,128,512]{2,1,0:T(8,128)(2,1)}, u32[]{:S(2)}) %copy-start) | copy-done | bytes 524312
  1.7 0.0 copy-start.1
  1.7 0.9 %copy-done.1 = bf16[24,4096]{1,0:T(8,128)(2,1)S(1)} copy-done((bf16[24,4096]{1,0:T(8,128)(2,1)S(1)}, bf16[24,4096]{1,0:T(8,128)(2,1)}, u32[]{:S(2)}) %copy-start.1) | copy-done | bytes 196632
  2.7 0.0 copy-start.2
  2.7 0.9 %copy-done.2 = bf16[256,256]{1,0:T(8,128)(2,1)S(1)} copy-done((bf16[256,256]{1,0:T(8,128)(2,1)S(1)}, bf16[256,256]{1,0:T(8,128)(2,1)}, u32[]{:S(2)}) %copy-start.2) | copy-done | bytes 131096
  3.6 73.3 %shard_map.64 = bf16[256,4,512]{2,1,0:T(4,128)(2,1)S(1)} custom-call(s32[1,192]{1,0:T(1,128)S(1)} %bitcast.5, bf16[512,512]{1,0:T(8,128)(2,1)S(1)} %bitcast.4, bf16[24,4096]{1,0:T(8,128)(2,1)S(1)} %copy-done.1, bf16[256,256]{1,0:T(8,128)(2,1)S(1)} %copy-done.2, s32[1,128]{1,0:T(1,128)S(1)} %bitcast.6, s32[1,128]{1,0:T(1,128)S(1)} %bitcast.7), custom_call_target="tpu_custom_call" | custom-call | flops 8000000000 | bytes 4000000 | tf_op jit(solution)/shard_map/pallas_call | solution.py:284
  76.9 1.0 %copy.8 = bf16[256,4,512]{2,1,0:T(4,128)(2,1)} copy(bf16[256,4,512]{2,1,0:T(4,128)(2,1)S(1)} %shard_map.64) | data formatting | bytes 2097152
Async XLA Ops:
  0.0 0.7 copy-start.5
  0.0 0.7 copy-start.3
  0.0 0.7 copy-start.4
  0.7 1.0 %copy-start = (bf16[4,128,512]{2,1,0:T(8,128)(2,1)S(1)}, bf16[4,128,512]{2,1,0:T(8,128)(2,1)}, u32[]{:S(2)}) copy-start(bf16[4,128,512]{2,1,0:T(8,128)(2,1)} %param.6) | copy-start | bytes 1572868
  1.7 0.9 %copy-start.1 = (bf16[24,4096]{1,0:T(8,128)(2,1)S(1)}, bf16[24,4096]{1,0:T(8,128)(2,1)}, u32[]{:S(2)}) copy-start(bf16[24,4096]{1,0:T(8,128)(2,1)} %int_ref.1) | copy-start | bytes 589828
  2.7 0.9 %copy-start.2 = (bf16[256,256]{1,0:T(8,128)(2,1)S(1)}, bf16[256,256]{1,0:T(8,128)(2,1)}, u32[]{:S(2)}) copy-start(bf16[256,256]{1,0:T(8,128)(2,1)} %hole_ref.1) | copy-start | bytes 393220
